TPU v7x, 256 devices: a whole 4x4x8 slice. The times are simulated.
256 devices in a mesh: samp: 32 (over z, y), rows: 8 (over x, core).
Axes of the slice: x: 4, y: 4, z: 8, core: 2. Of those that a mesh axis runs over, the one named last changes fastest.
Arguments:
- samples: float32 [32, 640, 4480], P('samp', 'rows'), may hold values from -6 to 6
- truth_field: float32 [640, 4480], P('rows', 'samp'), may hold values from -6 to 6
Outputs:
- contrast_fine: float32 [32, 640, 4480], P('samp', 'rows')
- contrast_half: float32 [32, 320, 2240], P('samp', 'rows')
- contrast_quarter: float32 [32, 160, 1120], P('samp', 'rows')
- contrast_eighth: float32 [32, 80, 560], P('samp', 'rows')
- similarity_coarse: float32 [32, 40, 280], P('samp', 'rows')
All inputs are finite; a program needn't handle non-finite values.
Results may differ from a plain program's by a relative error of at most 0.00002.
Values sent between devices are 32-bit elements; how exact they have to be, the bound alone decides.
No kernel may reach another device: no remote copies, remote signals or barrier semaphores. Data moves between devices by JAX's collectives and lax.ppermute only.
A program may use at most 128 MiB of HBM per device.

v0:
```python
import jax
import jax.numpy as jnp
from jax import lax
from jax.sharding import PartitionSpec as P

small_one = 0.0001
small_two = 0.0009


def with_halo(block, sides, width):
    for axis, dim in sides:
        count = lax.axis_size(axis)
        forward = [(i, i + 1) for i in range(count - 1)]
        backward = [(target, source) for source, target in forward]
        low = lax.ppermute(
            lax.slice_in_dim(block, block.shape[dim] - width, None, axis=dim), axis, forward
        )
        high = lax.ppermute(lax.slice_in_dim(block, 0, width, axis=dim), axis, backward)
        block = jnp.concatenate([low, block, high], axis=dim)
    return block


def window():
    offsets = jnp.arange(11).astype(jnp.float32) - 5.0
    shaped = jnp.exp(-offsets * offsets / 4.5)
    return shaped / jnp.sum(shaped)


def smooth(padded, weights):
    row_count = padded.shape[-2] - 10
    column_count = padded.shape[-1]
    vertical = weights[0] * padded[..., 0:row_count, :]
    for tap_index in range(1, 11):
        vertical = vertical + weights[tap_index] * padded[..., tap_index : tap_index + row_count, :]
    widths = [(0, 0)] * (padded.ndim - 1) + [(5, 5)]
    widened = jnp.pad(vertical, widths)
    result = weights[0] * widened[..., 0:column_count]
    for tap_index in range(1, 11):
        result = result + weights[tap_index] * widened[..., tap_index : tap_index + column_count]
    return result


def halve_grid(field):
    upper = field[..., 0::2, :]
    lower = field[..., 1::2, :]
    return 0.25 * (upper[..., 0::2] + upper[..., 1::2] + lower[..., 0::2] + lower[..., 1::2])


def level_maps(sample_pad, truth_pad, weights, coarsest):
    truth_wide = truth_pad[None]
    stacked = jnp.stack(
        [
            sample_pad,
            truth_wide,
            sample_pad * sample_pad,
            truth_wide * truth_wide,
            sample_pad * truth_wide,
        ],
        axis=0,
    )
    moments = lax.map(lambda field: smooth(field, weights), stacked)
    mean_x = moments[0]
    mean_y = moments[1]
    var_x = moments[2] - mean_x * mean_x
    var_y = moments[3] - mean_y * mean_y
    covar = moments[4] - mean_x * mean_y
    contrast = (2.0 * covar + small_two) / (var_x + var_y + small_two)
    if coarsest:
        luminance = (2.0 * mean_x * mean_y + small_one) / (
            mean_x * mean_x + mean_y * mean_y + small_one
        )
        return luminance * contrast
    return contrast


def local(samples, truth_field):
    weights = window()
    truth_levels = []
    sample_levels = []
    truth_rows = lax.all_gather(truth_field, "samp", axis=1, tiled=True)
    current = jnp.concatenate([truth_rows[None], samples], axis=0)
    for level_index in range(5):
        if level_index > 0:
            current = halve_grid(current)
        padded = with_halo(current, (("rows", 1),), 5)
        truth_levels.append(padded[0])
        sample_levels.append(padded[1:])
    return tuple(
        (
            level_maps(
                sample_levels[level_index], truth_levels[level_index], weights, level_index == 4
            )
            for level_index in range(5)
        )
    )


def solution(mesh):
    placed = (P("samp", "rows", None), P("rows", "samp"))
    return jax.shard_map(
        local,
        mesh=mesh,
        in_specs=placed,
        out_specs=(
            P("samp", "rows", None),
            P("samp", "rows", None),
            P("samp", "rows", None),
            P("samp", "rows", None),
            P("samp", "rows", None),
        ),
        check_vma=False,
    )
```

profile of v0, /device:TPU:1, one launch (start us, length us, event | category | flops | bytes accessed | tf_op | source)
XLA Modules:
  0.0 804.6 jit_solution(12436675204161090629)
XLA Ops:
  9.2 80.0 %all-gather.3.cloned.1.call-done = f32[32,140,80]{2,1,0:T(8,128)} async-done(((f32[1,140,80]{2,1,0:T(8,128)}), f32[32,140,80]{2,1,0:T(8,128)}) %all-gather.3.cloned.1.call-update) | async-done | bytes 1433616 | tf_op jit(solution)/shard_map/all_gather | solution.py:80
  103.6 30.2 %slice.1231 = f32[2,40,2240]{2,1,0:T(8,128)} slice(f32[2,40,4480]{2,1,0:T(8,128)} %slice.1230), slice={[0:2:1], [0:40:1], [0:4480:2]} | slice | bytes 1433600 | tf_op jit(solution)/shard_map/slice | solution.py:46
  133.8 30.2 %slice.1232 = f32[2,40,2240]{2,1,0:T(8,128)} slice(f32[2,40,4480]{2,1,0:T(8,128)} %slice.1230), slice={[0:2:1], [0:40:1], [1:4480:2]} | slice | bytes 1433600 | tf_op jit(solution)/shard_map/slice | solution.py:46
  171.6 30.4 %slice.1234 = f32[2,40,2240]{2,1,0:T(8,128)} slice(f32[2,40,4480]{2,1,0:T(8,128)} %slice.1233), slice={[0:2:1], [0:40:1], [0:4480:2]} | slice | bytes 1433600 | tf_op jit(solution)/shard_map/slice | solution.py:46
  201.9 30.2 %slice.1235 = f32[2,40,2240]{2,1,0:T(8,128)} slice(f32[2,40,4480]{2,1,0:T(8,128)} %slice.1233), slice={[0:2:1], [0:40:1], [1:4480:2]} | slice | bytes 1433600 | tf_op jit(solution)/shard_map/slice | solution.py:46
  304.2 80.6 %while.64 = (s32[]{:T(128)}, f32[5,1,5,280]{3,0,2,1:T(8,128)}, f32[11]{0:T(128)S(1)}, f32[5,1,15,280]{3,2,1,0:T(8,128)S(1)}, s32[]{:T(128)}, /*index=5*/s32[]{:T(128)}) while((s32[]{:T(128)}, f32[5,1,5,280]{3,0,2,1:T(8,128)}, f32[11]{0:T(128)S(1)}, f32[5,1,15,280]{3,2,1,0:T(8,128)S(1)}, s32[]{:T(128)}, /*index=5*/s32[]{:T(128)}) %tuple.190), condition=%wide.region_10.11_spmd, body=%wide.region_9.10_spmd.sunk | while | flops 58802 | bytes 134653 | solution.py:61
  392.2 83.3 %while.63 = (s32[]{:T(128)}, f32[5,1,10,560]{3,0,2,1:T(8,128)}, f32[11]{0:T(128)S(1)}, f32[5,1,20,560]{3,2,1,0:T(8,128)S(1)}, s32[]{:T(128)}, /*index=5*/s32[]{:T(128)}) while((s32[]{:T(128)}, f32[5,1,10,560]{3,0,2,1:T(8,128)}, f32[11]{0:T(128)S(1)}, f32[5,1,20,560]{3,2,1,0:T(8,128)S(1)}, s32[]{:T(128)}, /*index=5*/s32[]{:T(128)}) %tuple.195), condition=%wide.region_8.9_spmd, body=%wide.region_7.8_spmd.sunk | while | flops 235202 | bytes 493053 | solution.py:61
  481.6 94.7 %while.62 = (s32[]{:T(128)}, f32[5,1,20,1120]{3,0,2,1:T(8,128)}, f32[11]{0:T(128)S(1)}, f32[5,1,30,1120]{3,2,1,0:T(8,128)}, s32[]{:T(128)}, /*index=5*/s32[]{:T(128)}) while((s32[]{:T(128)}, f32[5,1,20,1120]{3,0,2,1:T(8,128)}, f32[11]{0:T(128)S(1)}, f32[5,1,30,1120]{3,2,1,0:T(8,128)}, s32[]{:T(128)}, /*index=5*/s32[]{:T(128)}) %tuple.201), condition=%wide.region_6.7_spmd, body=%wide.region_5.6_spmd.sunk | while | flops 940802 | bytes 1881853 | solution.py:61
  582.8 90.1 %while.61 = (s32[]{:T(128)}, f32[5,1,40,2240]{3,2,1,0:T(8,128)}, f32[11]{0:T(128)S(1)}, f32[5,1,50,2240]{3,2,1,0:T(8,128)}, s32[]{:T(128)}) while((s32[]{:T(128)}, f32[5,1,40,2240]{3,2,1,0:T(8,128)}, f32[11]{0:T(128)S(1)}, f32[5,1,50,2240]{3,2,1,0:T(8,128)}, s32[]{:T(128)}) %tuple.200), condition=%wide.region_4.5_spmd, body=%wide.region_3.4_spmd.sunk | while | flops 3763202 | bytes 5930181 | solution.py:61
  592.0 8.8 %bitcast_dynamic-update-slice_fusion.25 = f32[5,1,40,2240]{3,2,1,0:T(8,128)} fusion(f32[5,1,40,2240]{3,2,1,0:T(8,128)} %get-tuple-element.634, s32[]{:T(128)} %get-tuple-element.633, f32[1,40,2240]{2,1,0:T(8,128)S(1)} %fusion.123, f32[]{:T(128)} %bitcast.279, f32[]{:T(128)} %bitcast.280, f32[]{:T(128)} %bitcast.281, f32[]{:T(128)} %bitcast.282, ...), kind=kLoop, calls=%fused_computation.56.clone.1 | loop fusion | flops 1881600 | bytes 733184 | tf_op jit(solution)/shard_map/while/body/jit(dynamic_update_index_in_dim)/dynamic_update_slice | solution.py:61
  610.0 8.8 %bitcast_dynamic-update-slice_fusion.25 = f32[5,1,40,2240]{3,2,1,0:T(8,128)} fusion(f32[5,1,40,2240]{3,2,1,0:T(8,128)} %get-tuple-element.634, s32[]{:T(128)} %get-tuple-element.633, f32[1,40,2240]{2,1,0:T(8,128)S(1)} %fusion.123, f32[]{:T(128)} %bitcast.279, f32[]{:T(128)} %bitcast.280, f32[]{:T(128)} %bitcast.281, f32[]{:T(128)} %bitcast.282, ...), kind=kLoop, calls=%fused_computation.56.clone.1 | loop fusion | flops 1881600 | bytes 733184 | tf_op jit(solution)/shard_map/while/body/jit(dynamic_update_index_in_dim)/dynamic_update_slice | solution.py:61
  628.0 8.8 %bitcast_dynamic-update-slice_fusion.25 = f32[5,1,40,2240]{3,2,1,0:T(8,128)} fusion(f32[5,1,40,2240]{3,2,1,0:T(8,128)} %get-tuple-element.634, s32[]{:T(128)} %get-tuple-element.633, f32[1,40,2240]{2,1,0:T(8,128)S(1)} %fusion.123, f32[]{:T(128)} %bitcast.279, f32[]{:T(128)} %bitcast.280, f32[]{:T(128)} %bitcast.281, f32[]{:T(128)} %bitcast.282, ...), kind=kLoop, calls=%fused_computation.56.clone.1 | loop fusion | flops 1881600 | bytes 733184 | tf_op jit(solution)/shard_map/while/body/jit(dynamic_update_index_in_dim)/dynamic_update_slice | solution.py:61
  646.1 8.8 %bitcast_dynamic-update-slice_fusion.25 = f32[5,1,40,2240]{3,2,1,0:T(8,128)} fusion(f32[5,1,40,2240]{3,2,1,0:T(8,128)} %get-tuple-element.634, s32[]{:T(128)} %get-tuple-element.633, f32[1,40,2240]{2,1,0:T(8,128)S(1)} %fusion.123, f32[]{:T(128)} %bitcast.279, f32[]{:T(128)} %bitcast.280, f32[]{:T(128)} %bitcast.281, f32[]{:T(128)} %bitcast.282, ...), kind=kLoop, calls=%fused_computation.56.clone.1 | loop fusion | flops 1881600 | bytes 733184 | tf_op jit(solution)/shard_map/while/body/jit(dynamic_update_index_in_dim)/dynamic_update_slice | solution.py:61
  664.1 8.8 %bitcast_dynamic-update-slice_fusion.25 = f32[5,1,40,2240]{3,2,1,0:T(8,128)} fusion(f32[5,1,40,2240]{3,2,1,0:T(8,128)} %get-tuple-element.634, s32[]{:T(128)} %get-tuple-element.633, f32[1,40,2240]{2,1,0:T(8,128)S(1)} %fusion.123, f32[]{:T(128)} %bitcast.279, f32[]{:T(128)} %bitcast.280, f32[]{:T(128)} %bitcast.281, f32[]{:T(128)} %bitcast.282, ...), kind=kLoop, calls=%fused_computation.56.clone.1 | loop fusion | flops 1881600 | bytes 733184 | tf_op jit(solution)/shard_map/while/body/jit(dynamic_update_index_in_dim)/dynamic_update_slice | solution.py:61
  680.5 112.1 %while.60 = (s32[]{:T(128)}, f32[5,1,80,4480]{3,2,1,0:T(8,128)}, f32[11]{0:T(128)S(1)}, f32[5,1,90,4480]{3,2,1,0:T(8,128)}, s32[]{:T(128)}) while((s32[]{:T(128)}, f32[5,1,80,4480]{3,2,1,0:T(8,128)}, f32[11]{0:T(128)S(1)}, f32[5,1,90,4480]{3,2,1,0:T(8,128)}, s32[]{:T(128)}) %tuple.199), condition=%wide.region_2.3_spmd, body=%wide.region_1.2_spmd.sunk | while | flops 15052802 | bytes 23302340 | solution.py:61
  682.7 8.7 %fusion.121 = f32[1,80,4480]{2,1,0:T(8,128)S(1)} fusion(f32[1,90,4480]{2,1,0:T(8,128)S(1)} %dynamic-slice_bitcast_fusion.10, f32[]{:T(128)} %bitcast.266, f32[]{:T(128)} %bitcast.267, f32[]{:T(128)} %bitcast.268, f32[]{:T(128)} %bitcast.269, f32[]{:T(128)} %bitcast.270, f32[]{:T(128)} %bitcast.271, f32[]{:T(128)} %bitcast.272, f32[]{:T(128)} %bitcast.273, ...), kind=kLoop, calls=%fused_computation.2.clone.1 | loop fusion | flops 7526400 | bytes 17203244 | tf_op jit(solution)/shard_map/while/body/eval_jaxpr/add | solution.py:34
  691.4 11.5 %bitcast_dynamic-update-slice_fusion.24 = f32[5,1,80,4480]{3,2,1,0:T(8,128)} fusion(f32[5,1,80,4480]{3,2,1,0:T(8,128)} %get-tuple-element.619, s32[]{:T(128)} %get-tuple-element.618, f32[1,80,4480]{2,1,0:T(8,128)S(1)} %fusion.121, f32[]{:T(128)} %bitcast.266, f32[]{:T(128)} %bitcast.267, f32[]{:T(128)} %bitcast.268, f32[]{:T(128)} %bitcast.269, ...), kind=kLoop, calls=%fused_computation.22.clone.1 | loop fusion | flops 7526400 | bytes 2873344 | tf_op jit(solution)/shard_map/while/body/jit(dynamic_update_index_in_dim)/dynamic_update_slice | solution.py:61
  705.2 8.7 %fusion.121 = f32[1,80,4480]{2,1,0:T(8,128)S(1)} fusion(f32[1,90,4480]{2,1,0:T(8,128)S(1)} %dynamic-slice_bitcast_fusion.10, f32[]{:T(128)} %bitcast.266, f32[]{:T(128)} %bitcast.267, f32[]{:T(128)} %bitcast.268, f32[]{:T(128)} %bitcast.269, f32[]{:T(128)} %bitcast.270, f32[]{:T(128)} %bitcast.271, f32[]{:T(128)} %bitcast.272, f32[]{:T(128)} %bitcast.273, ...), kind=kLoop, calls=%fused_computation.2.clone.1 | loop fusion | flops 7526400 | bytes 17203244 | tf_op jit(solution)/shard_map/while/body/eval_jaxpr/add | solution.py:34
  713.9 11.5 %bitcast_dynamic-update-slice_fusion.24 = f32[5,1,80,4480]{3,2,1,0:T(8,128)} fusion(f32[5,1,80,4480]{3,2,1,0:T(8,128)} %get-tuple-element.619, s32[]{:T(128)} %get-tuple-element.618, f32[1,80,4480]{2,1,0:T(8,128)S(1)} %fusion.121, f32[]{:T(128)} %bitcast.266, f32[]{:T(128)} %bitcast.267, f32[]{:T(128)} %bitcast.268, f32[]{:T(128)} %bitcast.269, ...), kind=kLoop, calls=%fused_computation.22.clone.1 | loop fusion | flops 7526400 | bytes 2873344 | tf_op jit(solution)/shard_map/while/body/jit(dynamic_update_index_in_dim)/dynamic_update_slice | solution.py:61
  727.6 8.7 %fusion.121 = f32[1,80,4480]{2,1,0:T(8,128)S(1)} fusion(f32[1,90,4480]{2,1,0:T(8,128)S(1)} %dynamic-slice_bitcast_fusion.10, f32[]{:T(128)} %bitcast.266, f32[]{:T(128)} %bitcast.267, f32[]{:T(128)} %bitcast.268, f32[]{:T(128)} %bitcast.269, f32[]{:T(128)} %bitcast.270, f32[]{:T(128)} %bitcast.271, f32[]{:T(128)} %bitcast.272, f32[]{:T(128)} %bitcast.273, ...), kind=kLoop, calls=%fused_computation.2.clone.1 | loop fusion | flops 7526400 | bytes 17203244 | tf_op jit(solution)/shard_map/while/body/eval_jaxpr/add | solution.py:34
  736.3 11.5 %bitcast_dynamic-update-slice_fusion.24 = f32[5,1,80,4480]{3,2,1,0:T(8,128)} fusion(f32[5,1,80,4480]{3,2,1,0:T(8,128)} %get-tuple-element.619, s32[]{:T(128)} %get-tuple-element.618, f32[1,80,4480]{2,1,0:T(8,128)S(1)} %fusion.121, f32[]{:T(128)} %bitcast.266, f32[]{:T(128)} %bitcast.267, f32[]{:T(128)} %bitcast.268, f32[]{:T(128)} %bitcast.269, ...), kind=kLoop, calls=%fused_computation.22.clone.1 | loop fusion | flops 7526400 | bytes 2873344 | tf_op jit(solution)/shard_map/while/body/jit(dynamic_update_index_in_dim)/dynamic_update_slice | solution.py:61
  758.7 11.5 %bitcast_dynamic-update-slice_fusion.24 = f32[5,1,80,4480]{3,2,1,0:T(8,128)} fusion(f32[5,1,80,4480]{3,2,1,0:T(8,128)} %get-tuple-element.619, s32[]{:T(128)} %get-tuple-element.618, f32[1,80,4480]{2,1,0:T(8,128)S(1)} %fusion.121, f32[]{:T(128)} %bitcast.266, f32[]{:T(128)} %bitcast.267, f32[]{:T(128)} %bitcast.268, f32[]{:T(128)} %bitcast.269, ...), kind=kLoop, calls=%fused_computation.22.clone.1 | loop fusion | flops 7526400 | bytes 2873344 | tf_op jit(solution)/shard_map/while/body/jit(dynamic_update_index_in_dim)/dynamic_update_slice | solution.py:61
  772.5 8.7 %fusion.121 = f32[1,80,4480]{2,1,0:T(8,128)S(1)} fusion(f32[1,90,4480]{2,1,0:T(8,128)S(1)} %dynamic-slice_bitcast_fusion.10, f32[]{:T(128)} %bitcast.266, f32[]{:T(128)} %bitcast.267, f32[]{:T(128)} %bitcast.268, f32[]{:T(128)} %bitcast.269, f32[]{:T(128)} %bitcast.270, f32[]{:T(128)} %bitcast.271, f32[]{:T(128)} %bitcast.272, f32[]{:T(128)} %bitcast.273, ...), kind=kLoop, calls=%fused_computation.2.clone.1 | loop fusion | flops 7526400 | bytes 17203244 | tf_op jit(solution)/shard_map/while/body/eval_jaxpr/add | solution.py:34
  781.2 11.5 %bitcast_dynamic-update-slice_fusion.24 = f32[5,1,80,4480]{3,2,1,0:T(8,128)} fusion(f32[5,1,80,4480]{3,2,1,0:T(8,128)} %get-tuple-element.619, s32[]{:T(128)} %get-tuple-element.618, f32[1,80,4480]{2,1,0:T(8,128)S(1)} %fusion.121, f32[]{:T(128)} %bitcast.266, f32[]{:T(128)} %bitcast.267, f32[]{:T(128)} %bitcast.268, f32[]{:T(128)} %bitcast.269, ...), kind=kLoop, calls=%fused_computation.22.clone.1 | loop fusion | flops 7526400 | bytes 2873344 | tf_op jit(solution)/shard_map/while/body/jit(dynamic_update_index_in_dim)/dynamic_update_slice | solution.py:61
  (219 shorter events, 451.9 us)
Async XLA Ops:
  7.2 82.1 %all-gather.3.cloned.1.call-start = ((), (), s32[]{:S(2)}) async-start(), calls=%async_computation | async-start | bytes 2433024 | tf_op jit(solution)/shard_map/all_gather | solution.py:80
  92.0 2.3 copy-start
  277.0 21.6 %collective-permute-start.8 = (f32[2,5,280]{2,1,0:T(8,128)S(1)}, f32[2,5,280]{2,1,0:T(8,128)S(1)}, u32[]{:S(2)}, u32[]{:S(2)}) collective-permute-start(f32[2,5,280]{2,1,0:T(8,128)S(1)} %add_multiply_fusion.3), channel_id=1, source_target_pairs={{0,1},{1,2},{2,3},{3,4},{4,5},{5,6},{6,7},{8,9},{9,10},{10,11},{11... | collective-permute-start | bytes 33608 | tf_op jit(solution)/shard_map/ppermute | solution.py:15
  284.2 16.3 %collective-permute-start.9 = (f32[2,5,280]{2,1,0:T(8,128)S(1)}, f32[2,5,280]{2,1,0:T(8,128)S(1)}, u32[]{:S(2)}, u32[]{:S(2)}) collective-permute-start(f32[2,5,280]{2,1,0:T(8,128)S(1)} %add_multiply_fusion.3), channel_id=1, source_target_pairs={{1,0},{2,1},{3,2},{4,3},{5,4},{6,5},{7,6},{9,8},{10,9},{11,10},{12... | collective-permute-start | bytes 33608 | tf_op jit(solution)/shard_map/ppermute | solution.py:18
  289.3 97.2 %collective-permute-start.6 = (f32[2,5,560]{2,1,0:T(8,128)S(1)}, f32[2,5,560]{2,1,0:T(8,128)S(1)}, u32[]{:S(2)}, u32[]{:S(2)}) collective-permute-start(f32[2,5,560]{2,1,0:T(8,128)S(1)} %get-tuple-element.376), channel_id=1, source_target_pairs={{0,1},{1,2},{2,3},{3,4},{4,5},{5,6},{6,7},{8,9},{9,10},{10,11},{11... | collective-permute-start | bytes 67208 | tf_op jit(solution)/shard_map/ppermute | solution.py:15
  293.0 95.5 %collective-permute-start.7 = (f32[2,5,560]{2,1,0:T(8,128)S(1)}, f32[2,5,560]{2,1,0:T(8,128)S(1)}, u32[]{:S(2)}, u32[]{:S(2)}) collective-permute-start(f32[2,5,560]{2,1,0:T(8,128)S(1)} %get-tuple-element.377), channel_id=1, source_target_pairs={{1,0},{2,1},{3,2},{4,3},{5,4},{6,5},{7,6},{9,8},{10,9},{11,10},{12... | collective-permute-start | bytes 67208 | tf_op jit(solution)/shard_map/ppermute | solution.py:18
  294.9 182.8 %collective-permute-start.4 = (f32[2,5,1120]{2,1,0:T(8,128)}, f32[2,5,1120]{2,1,0:T(8,128)}, u32[]{:S(2)}, u32[]{:S(2)}) collective-permute-start(f32[2,5,1120]{2,1,0:T(8,128)} %get-tuple-element.374), channel_id=1, source_target_pairs={{0,1},{1,2},{2,3},{3,4},{4,5},{5,6},{6,7},{8,9},{9,10},{10,11},{11... | collective-permute-start | bytes 134408 | tf_op jit(solution)/shard_map/ppermute | solution.py:15
  298.6 181.0 %collective-permute-start.5 = (f32[2,5,1120]{2,1,0:T(8,128)S(1)}, f32[2,5,1120]{2,1,0:T(8,128)}, u32[]{:S(2)}, u32[]{:S(2)}) collective-permute-start(f32[2,5,1120]{2,1,0:T(8,128)S(1)} %get-tuple-element.375), channel_id=1, source_target_pairs={{1,0},{2,1},{3,2},{4,3},{5,4},{6,5},{7,6},{9,8},{10,9},{11,10},{12... | collective-permute-start | bytes 134408 | tf_op jit(solution)/shard_map/ppermute | solution.py:18
  300.5 279.2 %collective-permute-start.2 = (f32[2,5,2240]{2,1,0:T(8,128)}, f32[2,5,2240]{2,1,0:T(8,128)}, u32[]{:S(2)}, u32[]{:S(2)}) collective-permute-start(f32[2,5,2240]{2,1,0:T(8,128)} %get-tuple-element.372), channel_id=1, source_target_pairs={{0,1},{1,2},{2,3},{3,4},{4,5},{5,6},{6,7},{8,9},{9,10},{10,11},{11... | collective-permute-start | bytes 268808 | tf_op jit(solution)/shard_map/ppermute | solution.py:15
  386.5 193.2 %collective-permute-start.3 = (f32[2,5,2240]{2,1,0:T(8,128)}, f32[2,5,2240]{2,1,0:T(8,128)}, u32[]{:S(2)}, u32[]{:S(2)}) collective-permute-start(f32[2,5,2240]{2,1,0:T(8,128)} %get-tuple-element.373), channel_id=1, source_target_pairs={{1,0},{2,1},{3,2},{4,3},{5,4},{6,5},{7,6},{9,8},{10,9},{11,10},{12... | collective-permute-start | bytes 268808 | tf_op jit(solution)/shard_map/ppermute | solution.py:18
  388.4 286.8 %collective-permute-start = (f32[2,5,4480]{2,1,0:T(8,128)}, f32[2,5,4480]{2,1,0:T(8,128)}, u32[]{:S(2)}, u32[]{:S(2)}) collective-permute-start(f32[2,5,4480]{2,1,0:T(8,128)} %get-tuple-element.370), channel_id=1, source_target_pairs={{0,1},{1,2},{2,3},{3,4},{4,5},{5,6},{6,7},{8,9},{9,10},{10,11},{11... | collective-permute-start | bytes 537608 | tf_op jit(solution)/shard_map/ppermute | solution.py:15
  477.7 197.5 %collective-permute-start.1 = (f32[2,5,4480]{2,1,0:T(8,128)}, f32[2,5,4480]{2,1,0:T(8,128)S(1)}, u32[]{:S(2)}, u32[]{:S(2)}) collective-permute-start(f32[2,5,4480]{2,1,0:T(8,128)} %get-tuple-element.371), channel_id=1, source_target_pairs={{1,0},{2,1},{3,2},{4,3},{5,4},{6,5},{7,6},{9,8},{10,9},{11,10},{12... | collective-permute-start | bytes 537608 | tf_op jit(solution)/shard_map/ppermute | solution.py:18
  480.7 0.9 copy-start.3
  581.2 1.6 copy-start.2
  677.1 3.3 copy-start.1
Sparse Core Ops, SparseCore 0:
  10.6 78.6 all-gather.2
where the time goes:
time: 818 us; the launch traced here: 805 us
  other arithmetic  421 us (51%)
  local copies, waits for them, and re-layouts  256 us (31%)
  waiting for transfers between devices  80.7 us (10%)
  starting transfers between devices  31.4 us (4%)
  between operations  15 us (2%)
    add x25, other arithmetic, smooth(): vertical + weights[tap_index] * padded[..., tap_index:tap_index + row_cou...  185 us
    broadcast_in_dim x20, other arithmetic, level_maps(): moments = lax.map(lambda field: smooth(field, weights), stacked)  107 us
    dynamic_update_slice x10, other arithmetic, level_maps(): moments = lax.map(lambda field: smooth(field, weights), stacked)  101 us
    all_gather x1, waiting for transfers between devices, local(): truth_rows = lax.all_gather(truth_field, 'samp', axis=1, tiled=True)  80 us
    slice x4, local copies, waits for them, and re-layouts, halve_grid(): lower[..., 1::2]  39.5 us
    slice x4, local copies, waits for them, and re-layouts, halve_grid(): upper[..., 1::2]  39.1 us
    slice x4, local copies, waits for them, and re-layouts, halve_grid(): lower[..., 0::2]  39.1 us
    slice x4, local copies, waits for them, and re-layouts, halve_grid(): upper[..., 0::2] + upper[..., 1::2] + lower[..., 0::2] + lower[..., 1::2]  38.2 us
  transfers between devices with their start and end apart: 11, of which 1 were waited for; matrix products, arithmetic and copies ran while one was open for 45% of the time, Pallas kernels for 0%

commit v1 on v0

v1 whole, which is shorter than its diff:
```python
import functools

import jax
import jax.numpy as jnp
import numpy as np
from jax import lax
from jax.experimental import pallas as pl
from jax.experimental.pallas import tpu as pltpu
from jax.sharding import PartitionSpec as P

small_one = 0.0001
small_two = 0.0009

ROWS = (80, 40, 20, 10, 5)
COLS = (4480, 2240, 1120, 560, 280)
TILES = tuple(-(-c // 128) for c in COLS)
STRIPS = tuple(t + 1 for t in TILES)
HELD = (80, 48, 32, 16, 8)
POOLED = (80, 40, 24, 16, 8)
WORK = (80, 48, 32, 16, 16)
EDGE_AT = tuple(int(v) for v in np.cumsum((0,) + STRIPS))
EDGES = EDGE_AT[-1]
f32, bf16 = jnp.float32, jnp.bfloat16
VMEM = pl.BlockSpec(memory_space=pltpu.VMEM)
PARAMS = pltpu.CompilerParams(vmem_limit_bytes=56 * 1024 * 1024)


def window():
    offsets = np.arange(11).astype(np.float32) - np.float32(5.0)
    shaped = np.exp(-offsets * offsets / np.float32(4.5))
    return (shaped / shaped.sum(dtype=np.float32)).astype(np.float32)


TAPS = [float(v) for v in window()]


def split(value):
    high = value.astype(bf16)
    return high, (value - high.astype(f32)).astype(bf16)


def column_band():
    row = lax.broadcasted_iota(jnp.int32, (256, 128), 0)
    col = lax.broadcasted_iota(jnp.int32, (256, 128), 1)
    band = jnp.zeros((256, 128), f32)
    for tap in range(11):
        band = jnp.where(row - col == 59 + tap, TAPS[tap], band)
    return band


def pair_matrix():
    row = lax.broadcasted_iota(jnp.int32, (256, 128), 0)
    col = lax.broadcasted_iota(jnp.int32, (256, 128), 1)
    lane = jnp.where(row >= 128, row - 128, row)
    half = lane // 2
    side = jnp.where(lane >= 64, half - 32, half + 96)
    goal = jnp.where(row < 128, half + 32, side)
    return jnp.where(goal == col, 0.25, 0.0).astype(bf16)


def lanes(rows):
    return lax.broadcasted_iota(jnp.int32, (rows, 128), 1)


def pyramid(levels, low_ref, high_ref, pair_ref):
    pair_ref[...] = pair_matrix()
    for k in range(1, 5):
        src, dst = levels[k - 1], levels[k]
        rows = POOLED[k]
        pairs = pair_ref[...]
        lower = lanes(rows) < 64

        def rowsum(u):
            return src[u, pl.ds(0, rows, stride=2), :] + src[u, pl.ds(1, rows, stride=2), :]

        count = STRIPS[k - 1]
        for s in range(STRIPS[k]):
            zero = jnp.zeros((rows, 128), f32)
            middle = rowsum(2 * s) if 2 * s < count else zero
            left = rowsum(2 * s - 1) if 0 <= 2 * s - 1 < count else zero
            right = rowsum(2 * s + 1) if 2 * s + 1 < count else zero
            both = jnp.concatenate([middle, jnp.where(lower, right, left)], axis=1)
            first = both.astype(bf16)
            rest = both - first.astype(f32)
            second, third = split(rest)
            total = jnp.dot(third, pairs, preferred_element_type=f32)
            total += jnp.dot(second, pairs, preferred_element_type=f32)
            total += jnp.dot(first, pairs, preferred_element_type=f32)
            dst[s, 0:rows] = total
    for k in range(5):
        at, n, rows = EDGE_AT[k], STRIPS[k], ROWS[k]
        high_ref[at : at + n] = levels[k][:, 0:8, :]
        if rows >= 8:
            low_ref[at : at + n] = levels[k][:, rows - 8 : rows, :]
        else:
            low_ref[at : at + n, 0 : 8 - rows] = jnp.zeros((n, 8 - rows, 128), f32)
            low_ref[at : at + n, 8 - rows : 8] = levels[k][:, 0:rows, :]


def sample_kernel(x_ref, *refs):
    levels, low_ref, high_ref, pair_ref = refs[0:5], refs[5], refs[6], refs[7]
    lower = lanes(80) < 64
    before = jnp.zeros((80, 128), f32)
    for s in range(STRIPS[0]):
        now = jnp.zeros((80, 128), f32)
        if s < TILES[0]:
            now = pltpu.roll(x_ref[0, :, 128 * s : 128 * s + 128], 64, 1)
        levels[0][s] = jnp.where(lower, before, now)
        before = now
    pyramid(levels, low_ref, high_ref, pair_ref)


def pack_kernel(t_ref, out_ref):
    out_ref[0:80] = t_ref[:, 0:128]
    parts = [t_ref[8 * a : 8 * a + 8, 128:140] for a in range(10)]
    out_ref[80:88] = jnp.concatenate(parts + [jnp.zeros((8, 8), f32)], axis=1)


def truth_kernel(g_ref, *refs):
    levels, low_ref, high_ref, pair_ref = refs[0:5], refs[5], refs[6], refs[7]
    me = lax.axis_index("samp")
    my_z, my_y = me // 4, me % 4
    held = {}
    lane = lanes(80)
    for s in range(32):
        dz = lax.rem(my_z - s // 4 + 8, 8)
        dy = lax.rem(my_y - s % 4 + 4, 4)
        at = pl.multiple_of((dz * 4 + dy) * 88, 8)
        start = 64 + 140 * s
        q, off = start // 128, start % 128
        main = pltpu.roll(g_ref[pl.ds(at, 80), :], off, 1)
        tail8 = g_ref[pl.ds(pl.multiple_of(at + 80, 8), 8), :]
        tail = jnp.concatenate([pltpu.roll(tail8, (off - 12 * a) % 128, 1) for a in range(10)], axis=0)
        held.setdefault(q, []).append((main, off, 128))
        held.setdefault(q + 1, []).append((main, 0, off))
        held.setdefault(q + 1, []).append((tail, off, min(128, off + 12)))
        if off + 12 > 128:
            held.setdefault(q + 2, []).append((tail, 0, off + 12 - 128))
        last = 35 if s == 31 else (64 + 140 * (s + 1)) // 128 - 1
        for tile in sorted(held):
            if tile <= last:
                value = jnp.zeros((80, 128), f32)
                for piece, lo, hi in held.pop(tile):
                    if hi > lo:
                        value = jnp.where((lane >= lo) & (lane < hi), piece, value)
                levels[0][tile] = value
    pyramid(levels, low_ref, high_ref, pair_ref)


def maps_kernel(*refs):
    xs, ts = refs[0:5], refs[5:10]
    x_low, x_high, t_low, t_high = refs[10:14]
    outs = refs[14:19]
    band_ref, fine_ref, fields, v_high, v_low, v_full = refs[19:25]
    fine_ref[...] = column_band()
    high, low = split(fine_ref[...])
    band_ref[:, 0:128] = high
    band_ref[:, 128:256] = low
    for k in range(5):
        rows, held, work, at = ROWS[k], HELD[k], WORK[k], EDGE_AT[k]
        span = work + 16

        def vertical(s, slot):
            for field, (ref, low, high) in enumerate(((xs[k], x_low, x_high), (ts[k], t_low, t_high))):
                fields[field, 0:8] = low[at + s]
                fields[field, 8 : 8 + held] = ref[s]
                fields[field, 8 + rows : 16 + rows] = high[at + s]
            x, t = fields[0, 0:span], fields[1, 0:span]
            fields[2, 0:span] = x * x
            fields[3, 0:span] = t * t
            fields[4, 0:span] = x * t
            for field in range(5):
                total = TAPS[5] * fields[field, 8 : 8 + work]
                for tap in range(5):
                    pair = fields[field, 3 + tap : 3 + tap + work] + fields[field, 13 - tap : 13 - tap + work]
                    total = total + TAPS[tap] * pair
                if k >= 2:
                    v_full[slot, field * work : (field + 1) * work] = total
                    continue
                high, low = split(total)
                v_high[slot, field * work : (field + 1) * work] = high
                v_low[slot, field * work : (field + 1) * work] = low

        def finish(first, second, width):
            n = 5 * work
            if k >= 2:
                both = jnp.concatenate([v_full[first, 0:n], v_full[second, 0:n]], axis=1)
                acc = jnp.dot(
                    both, fine_ref[...], precision=lax.Precision.HIGHEST, preferred_element_type=f32
                )
                return ratio(acc)[:, 0:width]
            band = band_ref[...]
            both = jnp.concatenate([v_high[first, 0:n], v_high[second, 0:n]], axis=1)
            acc = jnp.dot(both, band, preferred_element_type=f32)
            both = jnp.concatenate([v_low[first, 0:n], v_low[second, 0:n]], axis=1)
            acc += jnp.dot(both, band, preferred_element_type=f32)
            return ratio(acc[:, 0:128] + acc[:, 128:256])[:, 0:width]

        def ratio(acc):
            mean_x, mean_y, second_x, second_y, cross = (
                acc[f * work : f * work + rows] for f in range(5)
            )
            square_x, square_y, product = mean_x * mean_x, mean_y * mean_y, mean_x * mean_y
            covar = cross - product
            result = (2.0 * covar + small_two) / (
                (second_x - square_x) + (second_y - square_y) + small_two
            )
            if k == 4:
                result = (2.0 * product + small_one) / (square_x + square_y + small_one) * result
            return result

        out, tiles = outs[k], TILES[k]
        whole = COLS[k] // 128
        vertical(0, 0)

        @pl.loop(0, whole)
        def _(j):
            odd = lax.rem(j, 2)
            vertical(j + 1, 1 - odd)
            out[0, :, pl.ds(pl.multiple_of(j * 128, 128), 128)] = finish(odd, 1 - odd, 128)

        if whole < tiles:
            odd = whole % 2
            vertical(tiles, 1 - odd)
            width = COLS[k] - 128 * whole
            out[0, :, 128 * whole :] = finish(odd, 1 - odd, width)


def level_shapes():
    return [jax.ShapeDtypeStruct((STRIPS[k], HELD[k], 128), f32) for k in range(5)] + [
        jax.ShapeDtypeStruct((EDGES, 8, 128), f32)
    ] * 2


def shifted(n, stride, k):
    perm = []
    for i in range(32):
        c = (i // stride) % n
        perm.append((i, i + ((c + k) % n - c) * stride))
    return perm


def along_z(x, k):
    return lax.ppermute(x, "samp", shifted(8, 4, k))


def along_y(x, k):
    return lax.ppermute(x, "samp", shifted(4, 1, k))


def gather(x):
    group = jnp.concatenate([x, along_y(x, 1), along_y(x, 2), along_y(x, -1)], axis=0)
    up, down = [group], [group]
    for _ in range(4):
        up.append(along_z(up[-1], 1))
    for _ in range(3):
        down.append(along_z(down[-1], -1))
    return jnp.concatenate(up + [down[3], down[2], down[1]], axis=0)


def local(samples, truth_field):
    forward = [(i, i + 1) for i in range(7)]
    backward = [(i + 1, i) for i in range(7)]
    scratch = [pltpu.VMEM((256, 128), bf16)]
    prepare = functools.partial(
        pl.pallas_call,
        out_shape=level_shapes(),
        in_specs=[VMEM],
        out_specs=[VMEM] * 7,
        scratch_shapes=scratch,
        compiler_params=PARAMS,
    )
    packed = pl.pallas_call(
        pack_kernel,
        out_shape=jax.ShapeDtypeStruct((88, 128), f32),
        in_specs=[VMEM],
        out_specs=VMEM,
        name="pack",
    )(truth_field)
    whole = gather(packed)
    cost = pl.CostEstimate(flops=10**9, bytes_accessed=10**7, transcendentals=0)
    *xs, x_low, x_high = prepare(sample_kernel, name="samples", cost_estimate=cost)(samples)
    x_low = lax.ppermute(x_low, "rows", forward)
    x_high = lax.ppermute(x_high, "rows", backward)
    *ts, t_low, t_high = prepare(truth_kernel, name="truth", cost_estimate=cost)(whole)
    t_low = lax.ppermute(t_low, "rows", forward)
    t_high = lax.ppermute(t_high, "rows", backward)
    return tuple(
        pl.pallas_call(
            maps_kernel,
            out_shape=[jax.ShapeDtypeStruct((1, ROWS[k], COLS[k]), f32) for k in range(5)],
            in_specs=[VMEM] * 14,
            out_specs=[VMEM] * 5,
            scratch_shapes=[
                pltpu.VMEM((256, 256), bf16),
                pltpu.VMEM((256, 128), f32),
                pltpu.VMEM((5, 96, 128), f32),
                pltpu.VMEM((2, 400, 128), bf16),
                pltpu.VMEM((2, 400, 128), bf16),
                pltpu.VMEM((2, 160, 128), f32),
            ],
            compiler_params=PARAMS,
            name="maps",
        )(*xs, *ts, x_low, x_high, t_low, t_high)
    )


def solution(mesh):
    placed = (P("samp", "rows", None), P("rows", "samp"))
    return jax.shard_map(
        local,
        mesh=mesh,
        in_specs=placed,
        out_specs=(P("samp", "rows", None),) * 5,
        check_vma=False,
    )
```

time: 818 us -> 99.9 us (0.12); the launches traced: 805 us -> 99.4 us
  other arithmetic: 421 us -> 0.8 us
  local copies, waits for them, and re-layouts: 256 us -> 7.89 us
  waiting for transfers between devices: 80.7 us -> 24 us
  Pallas kernels: 0 us -> 35.3 us
  between operations: 15 us -> 0.82 us
    slice x52 -> x0, local copies, waits for them, and re-layouts: 196 us -> none  [the longest x4 39.5 us: halve_grid(): lower[..., 1::2]]
    add x25 -> x0, other arithmetic: 185 us -> none  [smooth(): vertical + weights[tap_index] * padded[..., tap_index:tap_index + row_cou...]
    broadcast_in_dim x20 -> x0, other arithmetic: 107 us -> none  [level_maps(): moments = lax.map(lambda field: smooth(field, weights), stacked)]
    dynamic_update_slice x10 -> x0, other arithmetic: 101 us -> none  [level_maps(): moments = lax.map(lambda field: smooth(field, weights), stacked)]
    all_gather x1 -> x0, waiting for transfers between devices: 80 us -> none  [local(): truth_rows = lax.all_gather(truth_field, 'samp', axis=1, tiled=True)]
    pallas_call x0 -> x4, Pallas kernels: none -> 35.3 us  [the longest x1 26.3 us: local(): pl.pallas_call(maps_kernel, out_shape=[jax.ShapeDtypeStruct((1, ROWS[k],...]
    dynamic_update_slice x30 -> x0, local copies, waits for them, and re-layouts: 31.4 us -> none  [level_maps(): moments = lax.map(lambda field: smooth(field, weights), stacked)]
    ppermute x10 -> x14, waiting for transfers between devices: 0.03 us -> 24 us  [the longest x7 13.7 us: along_z(): return lax.ppermute(x, 'samp', shifted(8, 4, k))]
  transfers between devices with their start and end apart: 11 -> 14, of which waited for: 1 -> 10; matrix products, arithmetic and copies ran while one was open for 45% -> 0% of each run, Pallas kernels for 0% -> 8%
where the time goes in v1:
time: 99.9 us; the launch traced here: 99.4 us
  Pallas kernels  35.3 us (35%)
  starting transfers between devices  30.6 us (31%)
  waiting for transfers between devices  24 us (24%)
  local copies, waits for them, and re-layouts  7.89 us (8%)
    pallas_call x1, Pallas kernels, local(): pl.pallas_call(maps_kernel, out_shape=[jax.ShapeDtypeStruct((1, ROWS[k],...  26.3 us
    ppermute x7, waiting for transfers between devices, along_z(): return lax.ppermute(x, 'samp', shifted(8, 4, k))  13.7 us
    ppermute x7, starting transfers between devices, along_z(): return lax.ppermute(x, 'samp', shifted(8, 4, k))  11.7 us
    ppermute x1, starting transfers between devices, local(): x_low = lax.ppermute(x_low, 'rows', forward)  5.38 us
    ppermute x1, starting transfers between devices, local(): t_low = lax.ppermute(t_low, 'rows', forward)  4.86 us
    ppermute x3, starting transfers between devices, along_y(): return lax.ppermute(x, 'samp', shifted(4, 1, k))  4.6 us
    pallas_call x3, local copies, waits for them, and re-layouts, local(): pl.pallas_call(maps_kernel, out_shape=[jax.ShapeDtypeStruct((1, ROWS[k],...  4.35 us
    ppermute x1, waiting for transfers between devices, local(): t_high = lax.ppermute(t_high, 'rows', backward)  4.29 us
  transfers between devices with their start and end apart: 14, of which 10 were waited for; matrix products, arithmetic and copies ran while one was open for 0% of the time, Pallas kernels for 8%

profile of v1, /device:TPU:1, one launch (start us, length us, event | category | flops | bytes accessed | tf_op | source)
XLA Modules:
  0.0 99.4 jit_solution(4268539977404021564)
XLA Ops:
  0.6 1.6 %copy.7.t_ref = f32[80,140]{1,0:T(8,128)} copy(f32[80,140]{0,1:T(8,128)} %param.3) | data formatting | bytes 89600 | tf_op args[1]
  2.2 1.6 %pack.1 = f32[88,128]{1,0:T(8,128)} custom-call(f32[80,140]{1,0:T(8,128)} %copy.7.t_ref), custom_call_target="tpu_custom_call" | custom-call | tf_op jit(solution)/shard_map/pack/pallas_call | solution.py:273
  3.8 3.6 %collective-permute-start.2 = (f32[88,128]{1,0:T(8,128)}, f32[88,128]{1,0:T(8,128)S(1)}, u32[]{:S(2)}, u32[]{:S(2)}) collective-permute-start(f32[88,128]{1,0:T(8,128)} %pack.1), channel_id=1, source_target_pairs={{0,24},{8,0},{16,8},{24,16},{32,56},{40,32},{48,40},{56,48},{64,88... | collective-permute-start | bytes 135176 | tf_op jit(solution)/shard_map/ppermute | solution.py:248
  8.8 3.2 %collective-permute-done.1 = f32[88,128]{1,0:T(8,128)S(1)} collective-permute-done((f32[88,128]{1,0:T(8,128)}, f32[88,128]{1,0:T(8,128)S(1)}, u32[]{:S(2)}, u32[]{:S(2)}) %collective-permute-start.1) | collective-permute-done | bytes 45088 | tf_op jit(solution)/shard_map/ppermute | solution.py:248
  13.3 1.7 %collective-permute-start.3 = (f32[352,128]{1,0:T(8,128)S(1)}, f32[352,128]{1,0:T(8,128)S(1)}, u32[]{:S(2)}, u32[]{:S(2)}) collective-permute-start(f32[352,128]{1,0:T(8,128)S(1)} %pad_maximum_fusion), channel_id=1, source_target_pairs={{0,32},{8,40},{16,48},{24,56},{32,64},{40,72},{48,80},{56,88},{64,... | collective-permute-start | bytes 540680 | tf_op jit(solution)/shard_map/ppermute | solution.py:244
  15.0 3.5 %samples.1 = (f32[36,80,128]{2,1,0:T(8,128)}, f32[19,48,128]{2,1,0:T(8,128)}, f32[10,32,128]{2,1,0:T(8,128)}, f32[6,16,128]{2,1,0:T(8,128)}, f32[4,8,128]{2,1,0:...) custom-call(f32[1,80,4480]{2,1,0:T(8,128)} %x_ref.1), custom_call_target="tpu_custom_call" | custom-call | flops 1000000000 | bytes 10000000 | tf_op jit(solution)/shard_map/samples/pallas_call | solution.py:282
  18.5 5.4 %collective-permute-start.10 = (f32[75,8,128]{2,1,0:T(8,128)}, f32[75,8,128]{2,1,0:T(8,128)S(1)}, u32[]{:S(2)}, u32[]{:S(2)}) collective-permute-start(f32[75,8,128]{2,1,0:T(8,128)} %get-tuple-element.29), channel_id=1, source_target_pairs={{0,1},{1,2},{2,3},{3,4},{4,5},{5,6},{6,7},{8,9},{9,10},{10,11},{11... | collective-permute-start | bytes 921608 | tf_op jit(solution)/shard_map/ppermute | solution.py:283
  23.9 1.9 %collective-permute-start.11 = (f32[75,8,128]{2,1,0:T(8,128)}, f32[75,8,128]{2,1,0:T(8,128)S(1)}, u32[]{:S(2)}, u32[]{:S(2)}) collective-permute-start(f32[75,8,128]{2,1,0:T(8,128)} %get-tuple-element.30), channel_id=1, source_target_pairs={{1,0},{2,1},{3,2},{4,3},{5,4},{6,5},{7,6},{9,8},{10,9},{11,10},{12... | collective-permute-start | bytes 921608 | tf_op jit(solution)/shard_map/ppermute | solution.py:284
  25.9 3.8 %collective-permute-start.7 = (f32[352,128]{1,0:T(8,128)S(1)}, f32[352,128]{1,0:T(8,128)S(1)}, u32[]{:S(2)}, u32[]{:S(2)}) collective-permute-start(f32[352,128]{1,0:T(8,128)S(1)} %pad_maximum_fusion), channel_id=1, source_target_pairs={{0,224},{8,232},{16,240},{24,248},{32,0},{40,8},{48,16},{56,24},{6... | collective-permute-start | bytes 540680 | tf_op jit(solution)/shard_map/ppermute | solution.py:244
  29.7 2.5 %collective-permute-done.7 = f32[352,128]{1,0:T(8,128)S(1)} collective-permute-done((f32[352,128]{1,0:T(8,128)S(1)}, f32[352,128]{1,0:T(8,128)S(1)}, u32[]{:S(2)}, u32[]{:S(2)}) %collective-permute-start.7) | collective-permute-done | bytes 180256 | tf_op jit(solution)/shard_map/ppermute | solution.py:244
  32.1 3.1 %collective-permute-start.8 = (f32[352,128]{1,0:T(8,128)S(1)}, f32[352,128]{1,0:T(8,128)S(1)}, u32[]{:S(2)}, u32[]{:S(2)}) collective-permute-start(f32[352,128]{1,0:T(8,128)S(1)} %collective-permute-done.7), channel_id=1, source_target_pairs={{0,224},{8,232},{16,240},{24,248},{32,0},{40,8},{48,16},{56,24},{6... | collective-permute-start | bytes 540680 | tf_op jit(solution)/shard_map/ppermute | solution.py:244
  35.6 3.3 %collective-permute-done.8 = f32[352,128]{1,0:T(8,128)S(1)} collective-permute-done((f32[352,128]{1,0:T(8,128)S(1)}, f32[352,128]{1,0:T(8,128)S(1)}, u32[]{:S(2)}, u32[]{:S(2)}) %collective-permute-start.8) | collective-permute-done | bytes 180256 | tf_op jit(solution)/shard_map/ppermute | solution.py:244
  38.8 3.1 %collective-permute-start.9 = (f32[352,128]{1,0:T(8,128)S(1)}, f32[352,128]{1,0:T(8,128)S(1)}, u32[]{:S(2)}, u32[]{:S(2)}) collective-permute-start(f32[352,128]{1,0:T(8,128)S(1)} %collective-permute-done.8), channel_id=1, source_target_pairs={{0,224},{8,232},{16,240},{24,248},{32,0},{40,8},{48,16},{56,24},{6... | collective-permute-start | bytes 540680 | tf_op jit(solution)/shard_map/ppermute | solution.py:244
  42.6 7.1 %collective-permute-done.6 = f32[352,128]{1,0:T(8,128)S(1)} collective-permute-done((f32[352,128]{1,0:T(8,128)S(1)}, f32[352,128]{1,0:T(8,128)S(1)}, u32[]{:S(2)}, u32[]{:S(2)}) %collective-permute-start.6) | collective-permute-done | bytes 180256 | tf_op jit(solution)/shard_map/ppermute | solution.py:244
  49.7 1.1 %copy-done.5 = f32[2816,128]{1,0:T(8,128)} copy-done((f32[2816,128]{1,0:T(8,128)}, f32[2816,128]{1,0:T(8,128)S(1)}, u32[]{:S(2)}) %copy-start.5) | copy-done | bytes 1441816
  50.8 3.9 %truth.1 = (f32[36,80,128]{2,1,0:T(8,128)}, f32[19,48,128]{2,1,0:T(8,128)}, f32[10,32,128]{2,1,0:T(8,128)}, f32[6,16,128]{2,1,0:T(8,128)}, f32[4,8,128]{2,1,0:T(...) custom-call(f32[2816,128]{1,0:T(8,128)} %copy-done.5), custom_call_target="tpu_custom_call" | custom-call | flops 1000000000 | bytes 10000000 | tf_op jit(solution)/shard_map/truth/pallas_call | solution.py:285
  54.8 4.9 %collective-permute-start.12 = (f32[75,8,128]{2,1,0:T(8,128)}, f32[75,8,128]{2,1,0:T(8,128)S(1)}, u32[]{:S(2)}, u32[]{:S(2)}) collective-permute-start(f32[75,8,128]{2,1,0:T(8,128)} %get-tuple-element.31), channel_id=1, source_target_pairs={{0,1},{1,2},{2,3},{3,4},{4,5},{5,6},{6,7},{8,9},{9,10},{10,11},{11... | collective-permute-start | bytes 921608 | tf_op jit(solution)/shard_map/ppermute | solution.py:286
  59.6 2.1 %collective-permute-start.13 = (f32[75,8,128]{2,1,0:T(8,128)}, f32[75,8,128]{2,1,0:T(8,128)S(1)}, u32[]{:S(2)}, u32[]{:S(2)}) collective-permute-start(f32[75,8,128]{2,1,0:T(8,128)} %get-tuple-element.32), channel_id=1, source_target_pairs={{1,0},{2,1},{3,2},{4,3},{5,4},{6,5},{7,6},{9,8},{10,9},{11,10},{12... | collective-permute-start | bytes 921608 | tf_op jit(solution)/shard_map/ppermute | solution.py:287
  61.8 1.9 %collective-permute-done.12.refs_12_ = f32[75,8,128]{2,1,0:T(8,128)S(1)} collective-permute-done((f32[75,8,128]{2,1,0:T(8,128)}, f32[75,8,128]{2,1,0:T(8,128)S(1)}, u32[]{:S(2)}, u32[]{:S(2)}) %collective-permute-start.12) | collective-permute-done | bytes 307232 | tf_op jit(solution)/shard_map/ppermute | solution.py:286
  63.7 4.3 %collective-permute-done.13.refs_13_ = f32[75,8,128]{2,1,0:T(8,128)S(1)} collective-permute-done((f32[75,8,128]{2,1,0:T(8,128)}, f32[75,8,128]{2,1,0:T(8,128)S(1)}, u32[]{:S(2)}, u32[]{:S(2)}) %collective-permute-start.13) | collective-permute-done | bytes 307232 | tf_op jit(solution)/shard_map/ppermute | solution.py:287
  68.7 26.3 %maps.1 = (f32[1,80,4480]{2,1,0:T(8,128)}, f32[1,40,2240]{2,1,0:T(8,128)}, f32[1,20,1120]{2,1,0:T(8,128)}, f32[1,10,560]{2,1,0:T(8,128)}, f32[1,5,280]{2,1,0:T(8,128)}) custom-call(f32[36,80,128]{2,1,0:T(8,128)} %get-tuple-element.19.refs_0_, f32[19,48,128]{2,1,0:T(8,128)} %get-tuple-element.20.refs_1_, f32[10,32,128]{2,1,0:T(8,128)} %get-tuple-element.21.refs_2_, ...), custom_call_target="tpu_custom_call" | custom-call | tf_op jit(solution)/shard_map/maps/pallas_call | solution.py:289
  95.0 1.3 %copy.10 = f32[1,5,280]{2,0,1:T(1,128)} copy(f32[1,5,280]{2,1,0:T(8,128)} %get-tuple-element.37) | data formatting | bytes 11200 | tf_op jit(solution)/shard_map/maps/pallas_call | solution.py:289
  96.3 1.4 %copy.9 = f32[1,10,560]{2,0,1:T(1,128)} copy(f32[1,10,560]{2,1,0:T(8,128)} %get-tuple-element.36) | data formatting | bytes 44800 | tf_op jit(solution)/shard_map/maps/pallas_call | solution.py:289
  97.7 1.6 %copy.8 = f32[1,20,1120]{2,0,1:T(1,128)} copy(f32[1,20,1120]{2,1,0:T(8,128)} %get-tuple-element.35) | data formatting | bytes 179200 | tf_op jit(solution)/shard_map/maps/pallas_call | solution.py:289
  (36 shorter events, 4.4 us)
Async XLA Ops:
  3.8 5.0 %collective-permute-start.2 = (f32[88,128]{1,0:T(8,128)}, f32[88,128]{1,0:T(8,128)S(1)}, u32[]{:S(2)}, u32[]{:S(2)}) collective-permute-start(f32[88,128]{1,0:T(8,128)} %pack.1), channel_id=1, source_target_pairs={{0,24},{8,0},{16,8},{24,16},{32,56},{40,32},{48,40},{56,48},{64,88... | collective-permute-start | bytes 135176 | tf_op jit(solution)/shard_map/ppermute | solution.py:248
  7.4 4.7 %collective-permute-start.1 = (f32[88,128]{1,0:T(8,128)}, f32[88,128]{1,0:T(8,128)S(1)}, u32[]{:S(2)}, u32[]{:S(2)}) collective-permute-start(f32[88,128]{1,0:T(8,128)} %pack.1), channel_id=1, source_target_pairs={{0,16},{8,24},{16,0},{24,8},{32,48},{40,56},{48,32},{56,40},{64,80... | collective-permute-start | bytes 135176 | tf_op jit(solution)/shard_map/ppermute | solution.py:248
  7.7 4.7 %collective-permute-start = (f32[88,128]{1,0:T(8,128)}, f32[88,128]{1,0:T(8,128)S(1)}, u32[]{:S(2)}, u32[]{:S(2)}) collective-permute-start(f32[88,128]{1,0:T(8,128)} %pack.1), channel_id=1, source_target_pairs={{0,8},{8,16},{16,24},{24,0},{32,40},{40,48},{48,56},{56,32},{64,72... | collective-permute-start | bytes 135176 | tf_op jit(solution)/shard_map/ppermute | solution.py:248
  13.3 12.6 %copy-start = (f32[88,128]{1,0:T(8,128)S(1)}, f32[88,128]{1,0:T(8,128)}, u32[]{:S(2)}) copy-start(f32[88,128]{1,0:T(8,128)} %pack.1) | copy-start | bytes 135172
  13.3 16.3 %collective-permute-start.3 = (f32[352,128]{1,0:T(8,128)S(1)}, f32[352,128]{1,0:T(8,128)S(1)}, u32[]{:S(2)}, u32[]{:S(2)}) collective-permute-start(f32[352,128]{1,0:T(8,128)S(1)} %pad_maximum_fusion), channel_id=1, source_target_pairs={{0,32},{8,40},{16,48},{24,56},{32,64},{40,72},{48,80},{56,88},{64,... | collective-permute-start | bytes 540680 | tf_op jit(solution)/shard_map/ppermute | solution.py:244
  18.5 43.2 %collective-permute-start.10 = (f32[75,8,128]{2,1,0:T(8,128)}, f32[75,8,128]{2,1,0:T(8,128)S(1)}, u32[]{:S(2)}, u32[]{:S(2)}) collective-permute-start(f32[75,8,128]{2,1,0:T(8,128)} %get-tuple-element.29), channel_id=1, source_target_pairs={{0,1},{1,2},{2,3},{3,4},{4,5},{5,6},{6,7},{8,9},{9,10},{10,11},{11... | collective-permute-start | bytes 921608 | tf_op jit(solution)/shard_map/ppermute | solution.py:283
  23.9 37.8 %collective-permute-start.11 = (f32[75,8,128]{2,1,0:T(8,128)}, f32[75,8,128]{2,1,0:T(8,128)S(1)}, u32[]{:S(2)}, u32[]{:S(2)}) collective-permute-start(f32[75,8,128]{2,1,0:T(8,128)} %get-tuple-element.30), channel_id=1, source_target_pairs={{1,0},{2,1},{3,2},{4,3},{5,4},{6,5},{7,6},{9,8},{10,9},{11,10},{12... | collective-permute-start | bytes 921608 | tf_op jit(solution)/shard_map/ppermute | solution.py:284
  25.9 6.3 %collective-permute-start.7 = (f32[352,128]{1,0:T(8,128)S(1)}, f32[352,128]{1,0:T(8,128)S(1)}, u32[]{:S(2)}, u32[]{:S(2)}) collective-permute-start(f32[352,128]{1,0:T(8,128)S(1)} %pad_maximum_fusion), channel_id=1, source_target_pairs={{0,224},{8,232},{16,240},{24,248},{32,0},{40,8},{48,16},{56,24},{6... | collective-permute-start | bytes 540680 | tf_op jit(solution)/shard_map/ppermute | solution.py:244
  29.6 5.9 %collective-permute-start.4 = (f32[352,128]{1,0:T(8,128)S(1)}, f32[352,128]{1,0:T(8,128)S(1)}, u32[]{:S(2)}, u32[]{:S(2)}) collective-permute-start(f32[352,128]{1,0:T(8,128)S(1)} %collective-permute-done.3), channel_id=1, source_target_pairs={{0,32},{8,40},{16,48},{24,56},{32,64},{40,72},{48,80},{56,88},{64,... | collective-permute-start | bytes 540680 | tf_op jit(solution)/shard_map/ppermute | solution.py:244
  32.1 6.7 %collective-permute-start.8 = (f32[352,128]{1,0:T(8,128)S(1)}, f32[352,128]{1,0:T(8,128)S(1)}, u32[]{:S(2)}, u32[]{:S(2)}) collective-permute-start(f32[352,128]{1,0:T(8,128)S(1)} %collective-permute-done.7), channel_id=1, source_target_pairs={{0,224},{8,232},{16,240},{24,248},{32,0},{40,8},{48,16},{56,24},{6... | collective-permute-start | bytes 540680 | tf_op jit(solution)/shard_map/ppermute | solution.py:244
  35.5 7.0 %collective-permute-start.5 = (f32[352,128]{1,0:T(8,128)S(1)}, f32[352,128]{1,0:T(8,128)S(1)}, u32[]{:S(2)}, u32[]{:S(2)}) collective-permute-start(f32[352,128]{1,0:T(8,128)S(1)} %collective-permute-done.4), channel_id=1, source_target_pairs={{0,32},{8,40},{16,48},{24,56},{32,64},{40,72},{48,80},{56,88},{64,... | collective-permute-start | bytes 540680 | tf_op jit(solution)/shard_map/ppermute | solution.py:244
  38.8 10.8 %collective-permute-start.9 = (f32[352,128]{1,0:T(8,128)S(1)}, f32[352,128]{1,0:T(8,128)S(1)}, u32[]{:S(2)}, u32[]{:S(2)}) collective-permute-start(f32[352,128]{1,0:T(8,128)S(1)} %collective-permute-done.8), channel_id=1, source_target_pairs={{0,224},{8,232},{16,240},{24,248},{32,0},{40,8},{48,16},{56,24},{6... | collective-permute-start | bytes 540680 | tf_op jit(solution)/shard_map/ppermute | solution.py:244
  42.5 7.1 %collective-permute-start.6 = (f32[352,128]{1,0:T(8,128)S(1)}, f32[352,128]{1,0:T(8,128)S(1)}, u32[]{:S(2)}, u32[]{:S(2)}) collective-permute-start(f32[352,128]{1,0:T(8,128)S(1)} %collective-permute-done.5), channel_id=1, source_target_pairs={{0,32},{8,40},{16,48},{24,56},{32,64},{40,72},{48,80},{56,88},{64,... | collective-permute-start | bytes 540680 | tf_op jit(solution)/shard_map/ppermute | solution.py:244
  49.7 1.1 %copy-start.5 = (f32[2816,128]{1,0:T(8,128)}, f32[2816,128]{1,0:T(8,128)S(1)}, u32[]{:S(2)}) copy-start(f32[2816,128]{1,0:T(8,128)S(1)} %constant_dynamic-update-slice_fusion.g_ref) | copy-start | bytes 4325380
  54.8 9.0 %collective-permute-start.12 = (f32[75,8,128]{2,1,0:T(8,128)}, f32[75,8,128]{2,1,0:T(8,128)S(1)}, u32[]{:S(2)}, u32[]{:S(2)}) collective-permute-start(f32[75,8,128]{2,1,0:T(8,128)} %get-tuple-element.31), channel_id=1, source_target_pairs={{0,1},{1,2},{2,3},{3,4},{4,5},{5,6},{6,7},{8,9},{9,10},{10,11},{11... | collective-permute-start | bytes 921608 | tf_op jit(solution)/shard_map/ppermute | solution.py:286
  59.6 8.4 %collective-permute-start.13 = (f32[75,8,128]{2,1,0:T(8,128)}, f32[75,8,128]{2,1,0:T(8,128)S(1)}, u32[]{:S(2)}, u32[]{:S(2)}) collective-permute-start(f32[75,8,128]{2,1,0:T(8,128)} %get-tuple-element.32), channel_id=1, source_target_pairs={{1,0},{2,1},{3,2},{4,3},{5,4},{6,5},{7,6},{9,8},{10,9},{11,10},{12... | collective-permute-start | bytes 921608 | tf_op jit(solution)/shard_map/ppermute | solution.py:287
  61.8 6.3 %copy-start.1 = (f32[75,8,128]{2,1,0:T(8,128)}, f32[75,8,128]{2,1,0:T(8,128)S(1)}, u32[]{:S(2)}) copy-start(f32[75,8,128]{2,1,0:T(8,128)S(1)} %collective-permute-done.10.refs_10_) | copy-start | bytes 921604
  61.8 6.3 %copy-start.2 = (f32[75,8,128]{2,1,0:T(8,128)}, f32[75,8,128]{2,1,0:T(8,128)S(1)}, u32[]{:S(2)}) copy-start(f32[75,8,128]{2,1,0:T(8,128)S(1)} %collective-permute-done.11.refs_11_) | copy-start | bytes 921604
  63.7 4.3 %copy-start.3 = (f32[75,8,128]{2,1,0:T(8,128)}, f32[75,8,128]{2,1,0:T(8,128)S(1)}, u32[]{:S(2)}) copy-start(f32[75,8,128]{2,1,0:T(8,128)S(1)} %collective-permute-done.12.refs_12_) | copy-start | bytes 921604
  68.0 0.7 copy-start.4

commit v2 on v1

v2 whole, which is shorter than its diff:
```python
import functools

import jax
import jax.numpy as jnp
import numpy as np
from jax import lax
from jax.experimental import pallas as pl
from jax.experimental.pallas import tpu as pltpu
from jax.sharding import PartitionSpec as P

small_one = 0.0001
small_two = 0.0009

ROWS = (80, 40, 20, 10, 5)
COLS = (4480, 2240, 1120, 560, 280)
TILES = tuple(-(-c // 128) for c in COLS)
STRIPS = tuple(t + 1 for t in TILES)
HELD = (80, 48, 32, 16, 8)
POOLED = (80, 40, 24, 16, 8)
WORK = (80, 48, 32, 16, 16)
EDGE_AT = tuple(int(v) for v in np.cumsum((0,) + STRIPS))
EDGES = EDGE_AT[-1]
ORDER = (0, 1, 7, 3, 4, 2, 5, 6)
CHUNK = 9
f32, bf16 = jnp.float32, jnp.bfloat16
VMEM = pl.BlockSpec(memory_space=pltpu.VMEM)
ANYWHERE = pl.BlockSpec(memory_space=pl.ANY)
PARAMS = pltpu.CompilerParams(vmem_limit_bytes=20 * 1024 * 1024)


def window():
    offsets = np.arange(11).astype(np.float32) - np.float32(5.0)
    shaped = np.exp(-offsets * offsets / np.float32(4.5))
    return (shaped / shaped.sum(dtype=np.float32)).astype(np.float32)


TAPS = [float(v) for v in window()]


def split(value):
    high = value.astype(bf16)
    return high, (value - high.astype(f32)).astype(bf16)


def column_band():
    row = lax.broadcasted_iota(jnp.int32, (256, 128), 0)
    col = lax.broadcasted_iota(jnp.int32, (256, 128), 1)
    band = jnp.zeros((256, 128), f32)
    for tap in range(11):
        band = jnp.where(row - col == 59 + tap, TAPS[tap], band)
    return band


def pair_matrix():
    row = lax.broadcasted_iota(jnp.int32, (256, 128), 0)
    col = lax.broadcasted_iota(jnp.int32, (256, 128), 1)
    lane = jnp.where(row >= 128, row - 128, row)
    half = lane // 2
    side = jnp.where(lane >= 64, half - 32, half + 96)
    goal = jnp.where(row < 128, half + 32, side)
    return jnp.where(goal == col, 0.25, 0.0).astype(bf16)


def lanes(rows):
    return lax.broadcasted_iota(jnp.int32, (rows, 128), 1)


def pyramid(levels, low_ref, high_ref, pair_ref):
    pair_ref[...] = pair_matrix()
    for k in range(1, 5):
        src, dst = levels[k - 1], levels[k]
        rows = POOLED[k]
        pairs = pair_ref[...]
        lower = lanes(rows) < 64

        def rowsum(u):
            return src[u, pl.ds(0, rows, stride=2), :] + src[u, pl.ds(1, rows, stride=2), :]

        count = STRIPS[k - 1]
        for s in range(STRIPS[k]):
            zero = jnp.zeros((rows, 128), f32)
            middle = rowsum(2 * s) if 2 * s < count else zero
            left = rowsum(2 * s - 1) if 0 <= 2 * s - 1 < count else zero
            right = rowsum(2 * s + 1) if 2 * s + 1 < count else zero
            both = jnp.concatenate([middle, jnp.where(lower, right, left)], axis=1)
            first = both.astype(bf16)
            rest = both - first.astype(f32)
            second, third = split(rest)
            total = jnp.dot(third, pairs, preferred_element_type=f32)
            total += jnp.dot(second, pairs, preferred_element_type=f32)
            total += jnp.dot(first, pairs, preferred_element_type=f32)
            dst[s, 0:rows] = total
    for k in range(5):
        at, n, rows = EDGE_AT[k], STRIPS[k], ROWS[k]
        high_ref[at : at + n] = levels[k][:, 0:8, :]
        if rows >= 8:
            low_ref[at : at + n] = levels[k][:, rows - 8 : rows, :]
        else:
            low_ref[at : at + n, 0 : 8 - rows] = jnp.zeros((n, 8 - rows, 128), f32)
            low_ref[at : at + n, 8 - rows : 8] = levels[k][:, 0:rows, :]


def sample_kernel(x_ref, *refs):
    levels, low_ref, high_ref, pair_ref = refs[0:5], refs[5], refs[6], refs[7]
    lower = lanes(80) < 64
    before = jnp.zeros((80, 128), f32)
    for s in range(STRIPS[0]):
        now = jnp.zeros((80, 128), f32)
        if s < TILES[0]:
            now = pltpu.roll(x_ref[0, :, 128 * s : 128 * s + 128], 64, 1)
        levels[0][s] = jnp.where(lower, before, now)
        before = now
    pyramid(levels, low_ref, high_ref, pair_ref)


def pack_kernel(t_ref, out_ref):
    out_ref[0:80] = t_ref[0:128, :].T
    rest = t_ref[128:140, :].T
    parts = [rest[8 * a : 8 * a + 8] for a in range(10)]
    out_ref[80:88] = jnp.concatenate(parts + [jnp.zeros((8, 8), f32)], axis=1)


def truth_kernel(g_ref, *refs):
    refs = refs[2:]
    levels, low_ref, high_ref, pair_ref = refs[0:5], refs[5], refs[6], refs[7]
    me = lax.axis_index("samp")
    my_z, my_y = me // 4, me % 4
    held = {}
    lane = lanes(80)
    for s in range(32):
        dz = lax.rem(my_z - s // 4 + 8, 8)
        slot = dz
        for apart in (2, 5, 6, 7):
            slot = jnp.where(dz == apart, ORDER.index(apart), slot)
        dy = lax.rem(my_y - s % 4 + 4, 4)
        at = pl.multiple_of((dy * 8 + slot) * 88, 8)
        start = 64 + 140 * s
        q, off = start // 128, start % 128
        main = pltpu.roll(g_ref[pl.ds(at, 80), :], off, 1)
        tail8 = g_ref[pl.ds(pl.multiple_of(at + 80, 8), 8), :]
        tail = jnp.concatenate([pltpu.roll(tail8, (off - 12 * a) % 128, 1) for a in range(10)], axis=0)
        held.setdefault(q, []).append((main, off, 128))
        held.setdefault(q + 1, []).append((main, 0, off))
        held.setdefault(q + 1, []).append((tail, off, min(128, off + 12)))
        if off + 12 > 128:
            held.setdefault(q + 2, []).append((tail, 0, off + 12 - 128))
        last = 35 if s == 31 else (64 + 140 * (s + 1)) // 128 - 1
        for tile in sorted(held):
            if tile <= last:
                value = jnp.zeros((80, 128), f32)
                for piece, lo, hi in held.pop(tile):
                    if hi > lo:
                        value = jnp.where((lane >= lo) & (lane < hi), piece, value)
                levels[0][tile] = value
    pyramid(levels, low_ref, high_ref, pair_ref)


def set_bands(band_ref, fine_ref=None):
    band = column_band()
    high, low = split(band)
    band_ref[:, 0:128] = high
    band_ref[:, 128:256] = low
    if fine_ref is not None:
        fine_ref[...] = band


def row_sum(read, work):
    total = TAPS[5] * read(5, work)
    for tap in range(5):
        total = total + TAPS[tap] * (read(tap, work) + read(10 - tap, work))
    return total


def keep(at, slot, v_high, v_low, total):
    high, low = split(total)
    n = total.shape[0]
    v_high[slot, at : at + n] = high
    v_low[slot, at : at + n] = low


def column_sum(first, second, n, v_high, v_low, band_ref):
    band = band_ref[...]
    both = jnp.concatenate([v_high[first, 0:n], v_high[second, 0:n]], axis=1)
    acc = jnp.dot(both, band, preferred_element_type=f32)
    both = jnp.concatenate([v_low[first, 0:n], v_low[second, 0:n]], axis=1)
    acc += jnp.dot(both, band, preferred_element_type=f32)
    return acc[:, 0:128] + acc[:, 128:256]


def fine_sum(first, second, n, v_full, fine_ref):
    both = jnp.concatenate([v_full[first, 0:n], v_full[second, 0:n]], axis=1)
    return jnp.dot(
        both, fine_ref[...], precision=lax.Precision.HIGHEST, preferred_element_type=f32
    )


def ratio(mean_x, var_x, mean_y, second_y, cross, coarsest=False):
    square_y, product = mean_y * mean_y, mean_x * mean_y
    result = (2.0 * (cross - product) + small_two) / (
        var_x + (second_y - square_y) + small_two
    )
    if coarsest:
        result = (2.0 * product + small_one) / (mean_x * mean_x + square_y + small_one) * result
    return result


def fine_x_kernel(x_ref, x_next, low_ref, low_next, high_ref, high_next, mean_ref, var_ref, *scratch):
    band_ref, fields, v_high, v_low = scratch

    def vertical(x, low, high, slot):
        at = 2 * (slot % 3)
        fields[at, 0:8] = low
        fields[at, 8:88] = x
        fields[at, 88:96] = high
        whole = fields[at]
        fields[at + 1] = whole * whole
        for f in range(2):
            keep(80 * f, slot, v_high, v_low, row_sum(lambda i, n: fields[at + f, 3 + i : 3 + i + n], 80))

    def finish(j):
        acc = column_sum(j, j + 1, 160, v_high, v_low, band_ref)
        mean = acc[0:80]
        mean_ref[j] = mean
        var_ref[j] = acc[80:160] - mean * mean

    @pl.when(pl.program_id(0) == 0)
    def _():
        set_bands(band_ref)
        vertical(x_ref[0], low_ref[0], high_ref[0], 0)

    @pl.when(pl.program_id(0) > 0)
    def _():
        v_high[0] = v_high[CHUNK]
        v_low[0] = v_low[CHUNK]

    for j in range(CHUNK - 1):
        vertical(x_ref[j + 1], low_ref[j + 1], high_ref[j + 1], j + 1)
        finish(j)
    vertical(x_next[0], low_next[0], high_next[0], CHUNK)
    finish(CHUNK - 1)


def fine_t_kernel(x_ref, x_next, t_ref, t_next, mean_ref, var_ref, out_ref, *scratch):
    band_ref, fields, v_high, v_low = scratch

    def vertical(x, t, slot):
        at = 2 * (slot % 3)
        tv = t[...]
        fields[at] = tv * tv
        fields[at + 1] = x[...] * tv
        keep(0, slot, v_high, v_low, row_sum(lambda i, n: t[3 + i : 3 + i + n], 64))
        for f in range(2):
            total = row_sum(lambda i, n: fields[at + f, 3 + i : 3 + i + n], 64)
            keep(64 * f + 64, slot, v_high, v_low, total)

    def finish(j):
        acc = column_sum(j, j + 1, 192, v_high, v_low, band_ref)
        out_ref[0, 8:72, j * 128 : j * 128 + 128] = ratio(
            mean_ref[j, 8:72], var_ref[j, 8:72], acc[0:64], acc[64:128], acc[128:192]
        )

    @pl.when(pl.program_id(0) == 0)
    def _():
        set_bands(band_ref)
        vertical(x_ref.at[0], t_ref.at[0], 0)

    @pl.when(pl.program_id(0) > 0)
    def _():
        v_high[0] = v_high[CHUNK]
        v_low[0] = v_low[CHUNK]

    for j in range(CHUNK - 1):
        vertical(x_ref.at[j + 1], t_ref.at[j + 1], j + 1)
        finish(j)
    vertical(x_next.at[0], t_next.at[0], CHUNK)
    finish(CHUNK - 1)


def fill(fields, field, ref, low, high, k, s):
    at = EDGE_AT[k] + s
    fields[field, 0:8] = low[at]
    fields[field, 8 : 8 + HELD[k]] = ref[s]
    fields[field, 8 + ROWS[k] : 16 + ROWS[k]] = high[at]


def coarse_x_kernel(*refs):
    xs, (low, high), means, variances = refs[0:4], refs[4:6], refs[6:10], refs[10:14]
    band_ref, fine_ref, fields, v_high, v_low, v_full = refs[14:20]
    set_bands(band_ref, fine_ref)
    for k in range(1, 5):
        rows, work = ROWS[k], WORK[k]
        span = work + 16

        def vertical(s, slot):
            at = 2 * slot
            fill(fields, at, xs[k - 1], low, high, k, s)
            x = fields[at, 0:span]
            fields[at + 1, 0:span] = x * x
            for f in range(2):
                total = row_sum(lambda i, n: fields[at + f, 3 + i : 3 + i + n], work)
                if k >= 2:
                    v_full[slot, f * work : (f + 1) * work] = total
                else:
                    keep(f * work, slot, v_high, v_low, total)

        def finish(j, slot):
            if k >= 2:
                acc = fine_sum(slot, (slot + 1) % 3, 2 * work, v_full, fine_ref)
            else:
                acc = column_sum(slot, (slot + 1) % 3, 2 * work, v_high, v_low, band_ref)
            mean = acc[0:work]
            means[k - 1][j] = mean
            variances[k - 1][j] = acc[work : 2 * work] - mean * mean

        vertical(0, 0)

        for j in range(TILES[k]):
            vertical(j + 1, (j + 1) % 3)
            finish(j, j % 3)


def coarse_t_kernel(*refs):
    xs, ts = refs[0:4], refs[4:8]
    x_low, x_high, t_low, t_high = refs[8:12]
    means, variances = refs[12:16], refs[16:20]
    x_ends, t_ends, mean_ends, var_ends = refs[20:22], refs[22:24], refs[24:26], refs[26:28]
    out_fine, outs = refs[29], refs[30:34]
    band_ref, fine_ref, fields, v_high, v_low, v_full, ends, sems = refs[34:42]
    set_bands(band_ref, fine_ref)

    def rows_of(f, start):
        return lambda i, n: fields[f, start + 3 + i : start + 3 + i + n]

    def vertical(s, slot):
        for f, (two, low, high) in enumerate(((t_ends, t_low, t_high), (x_ends, x_low, x_high))):
            fields[3 * slot + f, 0:8] = low[s]
            fields[3 * slot + f, 8:24] = two[0][s]
            fields[3 * slot + f, 24:40] = two[1][s]
            fields[3 * slot + f, 40:48] = high[s]
        t, x = fields[3 * slot, 0:48], fields[3 * slot + 1, 0:48]
        fields[3 * slot + 1, 0:48] = t * t
        fields[3 * slot + 2, 0:48] = x * t
        for f in range(3):
            top = row_sum(rows_of(3 * slot + f, 0), 8)
            bottom = row_sum(rows_of(3 * slot + f, 24), 8)
            keep(16 * f, slot, v_high, v_low, jnp.concatenate([top, bottom], axis=0))

    def finish(j, slot):
        acc = column_sum(slot, (slot + 1) % 3, 48, v_high, v_low, band_ref)
        for end in range(2):
            at = 8 * end
            ends[end, :, j * 128 : j * 128 + 128] = ratio(
                mean_ends[end][j],
                var_ends[end][j],
                acc[at : at + 8],
                acc[16 + at : 24 + at],
                acc[32 + at : 40 + at],
            )

    vertical(0, 0)

    for j in range(TILES[0]):
        vertical(j + 1, (j + 1) % 3)
        finish(j, j % 3)

    copies = [
        pltpu.make_async_copy(ends.at[end], out_fine.at[0, pl.ds(72 * end, 8), :], sems.at[end])
        for end in range(2)
    ]
    for copy in copies:
        copy.start()

    for k in range(1, 5):
        rows, work = ROWS[k], WORK[k]
        span = work + 16

        def vertical(s, slot):
            at = 3 * slot
            fill(fields, at, ts[k - 1], t_low, t_high, k, s)
            fill(fields, at + 1, xs[k - 1], x_low, x_high, k, s)
            t, x = fields[at, 0:span], fields[at + 1, 0:span]
            fields[at + 1, 0:span] = t * t
            fields[at + 2, 0:span] = x * t
            for f in range(3):
                total = row_sum(rows_of(at + f, 0), work)
                if k >= 2:
                    v_full[slot, f * work : (f + 1) * work] = total
                else:
                    keep(f * work, slot, v_high, v_low, total)

        def finish(j, slot, width):
            if k >= 2:
                acc = fine_sum(slot, (slot + 1) % 3, 3 * work, v_full, fine_ref)
            else:
                acc = column_sum(slot, (slot + 1) % 3, 3 * work, v_high, v_low, band_ref)
            parts = (acc[f * work : f * work + rows] for f in range(3))
            value = ratio(means[k - 1][j, 0:rows], variances[k - 1][j, 0:rows], *parts, k == 4)
            return value[:, 0:width]

        out, tiles = outs[k - 1], TILES[k]
        whole = COLS[k] // 128
        vertical(0, 0)

        for j in range(tiles):
            vertical(j + 1, (j + 1) % 3)
            cols = pl.ds(128 * j, 128 if j < whole else COLS[k] - 128 * whole)
            if k == 1:
                out[0, :, cols] = finish(j, j % 3, cols.size)
            else:
                out[:, 0, cols] = finish(j, j % 3, cols.size)

    for copy in copies:
        copy.wait()


def level_shapes():
    return [jax.ShapeDtypeStruct((STRIPS[k], HELD[k], 128), f32) for k in range(5)] + [
        jax.ShapeDtypeStruct((EDGES, 8, 128), f32)
    ] * 2


def shifted(n, stride, k):
    perm = []
    for i in range(32):
        c = (i // stride) % n
        perm.append((i, i + ((c + k) % n - c) * stride))
    return perm


def along_z(x, k):
    return lax.ppermute(x, "samp", shifted(8, 4, k))


def along_y(x, k):
    return lax.ppermute(x, "samp", shifted(4, 1, k))


def join_kernel(*refs):
    out_ref = refs[-1]
    at = 0
    for ref in refs[:-2]:
        n = ref.shape[0]
        out_ref[at : at + n] = ref[...]
        at += n


def join(parts, before):
    rows = sum(part.shape[0] for part in parts)
    return pl.pallas_call(
        join_kernel,
        out_shape=jax.ShapeDtypeStruct((rows, 128), f32),
        in_specs=[VMEM] * len(parts) + [ANYWHERE],
        out_specs=VMEM,
        compiler_params=PARAMS,
        cost_estimate=cost(0.02),
        name="join",
    )(*parts, before)


def cut(column, half, before):
    n = column.shape[0] // 2
    return pl.pallas_call(
        lambda ref, _, out_ref: join_kernel(ref, _, out_ref),
        grid=(1,),
        out_shape=jax.ShapeDtypeStruct((n, 128), f32),
        in_specs=[pl.BlockSpec((n, 128), lambda g: (half, 0)), ANYWHERE],
        out_specs=VMEM,
        compiler_params=PARAMS,
        cost_estimate=cost(0.02),
        name="cut",
    )(column, before)


def chunk_spec(rows, base, step=None):
    if step is None:
        return pl.BlockSpec((CHUNK, rows, 128), lambda g: (g + base, 0, 0))
    return pl.BlockSpec(
        (1, rows, 128), lambda g: (jnp.minimum((g + base + 1) * CHUNK, STRIPS[0] - 1), 0, 0)
    )


def both_specs(rows, base):
    return [chunk_spec(rows, base), chunk_spec(rows, base, 1)]


def cost(micros):
    return pl.CostEstimate(flops=0, bytes_accessed=int(micros * 5e7), transcendentals=0)


def fine_x(x, low, high, *before):
    return pl.pallas_call(
        lambda *refs: fine_x_kernel(*refs[0:6], *refs[6 + len(before) :]),
        grid=(STRIPS[0] // CHUNK,),
        out_shape=[jax.ShapeDtypeStruct((STRIPS[0], 80, 128), f32)] * 2,
        in_specs=both_specs(80, 0) + both_specs(8, 0) + both_specs(8, 0) + [ANYWHERE] * len(before),
        out_specs=[chunk_spec(80, 0)] * 2,
        scratch_shapes=[
            pltpu.VMEM((256, 256), bf16),
            pltpu.VMEM((6, 96, 128), f32),
            pltpu.VMEM((CHUNK + 1, 160, 128), bf16),
            pltpu.VMEM((CHUNK + 1, 160, 128), bf16),
        ],
        compiler_params=PARAMS,
        cost_estimate=cost(5),
        name="fine_x",
    )(x, x, low, low, high, high, *before)


def coarse_x(xs, low, high, *before):
    shapes = [jax.ShapeDtypeStruct((TILES[k], WORK[k], 128), f32) for k in range(1, 5)]
    return pl.pallas_call(
        lambda *refs: coarse_x_kernel(*refs[0:6], *refs[6 + len(before) :]),
        out_shape=shapes * 2,
        in_specs=[VMEM] * 6 + [ANYWHERE] * len(before),
        out_specs=[VMEM] * 8,
        scratch_shapes=[
            pltpu.VMEM((256, 256), bf16),
            pltpu.VMEM((256, 128), f32),
            pltpu.VMEM((6, 64, 128), f32),
            pltpu.VMEM((3, 96, 128), bf16),
            pltpu.VMEM((3, 96, 128), bf16),
            pltpu.VMEM((3, 64, 128), f32),
        ],
        compiler_params=PARAMS,
        cost_estimate=cost(5),
        name="coarse_x",
    )(*xs[1:], low, high, *before)


def fine_t(x, t, mean, var):
    return pl.pallas_call(
        fine_t_kernel,
        grid=(STRIPS[0] // CHUNK,),
        out_shape=jax.ShapeDtypeStruct((1, 80, COLS[0]), f32),
        in_specs=both_specs(80, 0) + both_specs(80, 0) + [chunk_spec(80, 0)] * 2,
        out_specs=pl.BlockSpec((1, 80, 128 * CHUNK), lambda g: (0, 0, g)),
        scratch_shapes=[
            pltpu.VMEM((256, 256), bf16),
            pltpu.VMEM((6, 80, 128), f32),
            pltpu.VMEM((CHUNK + 1, 192, 128), bf16),
            pltpu.VMEM((CHUNK + 1, 192, 128), bf16),
        ],
        compiler_params=PARAMS,
        cost_estimate=cost(8),
        name="fine_t",
    )(x, x, t, t, mean, var)


def coarse_t(xs, ts, edges, coarse, mean, var, fine):
    def ends(rows, last):
        return [
            pl.BlockSpec((STRIPS[0], rows, 128), lambda g: (0, 0, 0)),
            pl.BlockSpec((STRIPS[0], rows, 128), lambda g: (0, last, 0)),
        ]

    shapes = [jax.ShapeDtypeStruct((1, 80, COLS[0]), f32), jax.ShapeDtypeStruct((1, 40, COLS[1]), f32)]
    shapes += [jax.ShapeDtypeStruct((ROWS[k], 1, COLS[k]), f32) for k in range(2, 5)]
    fine, half, *rest = pl.pallas_call(
        coarse_t_kernel,
        grid=(1,),
        out_shape=shapes,
        in_specs=[VMEM] * 20 + ends(16, 4) * 2 + ends(8, 9) * 2 + [ANYWHERE],
        out_specs=[ANYWHERE] + [VMEM] * 4,
        input_output_aliases={28: 0},
        scratch_shapes=[
            pltpu.VMEM((256, 256), bf16),
            pltpu.VMEM((256, 128), f32),
            pltpu.VMEM((9, 64, 128), f32),
            pltpu.VMEM((3, 144, 128), bf16),
            pltpu.VMEM((3, 144, 128), bf16),
            pltpu.VMEM((3, 96, 128), f32),
            pltpu.VMEM((2, 8, COLS[0]), f32),
            pltpu.SemaphoreType.DMA((2,)),
        ],
        compiler_params=PARAMS,
        name="coarse_t",
    )(*xs[1:], *ts[1:], *edges, *coarse, xs[0], xs[0], ts[0], ts[0], mean, mean, var, var, fine)
    return (fine, half) + tuple(value.transpose(1, 0, 2) for value in rest)


def local(samples, truth_field):
    forward = [(i, i + 1) for i in range(7)]
    backward = [(i + 1, i) for i in range(7)]
    prepare = functools.partial(
        pl.pallas_call,
        out_shape=level_shapes(),
        in_specs=[VMEM],
        out_specs=[VMEM] * 7,
        scratch_shapes=[pltpu.VMEM((256, 128), bf16)],
        compiler_params=PARAMS,
        cost_estimate=cost(4),
    )
    packed = pl.pallas_call(
        pack_kernel,
        out_shape=jax.ShapeDtypeStruct((88, 128), f32),
        in_specs=[VMEM],
        out_specs=VMEM,
        name="pack",
    )(truth_field.T)
    three = jnp.concatenate([packed, along_z(packed, 1), along_z(packed, -1)], axis=0)
    far = [along_z(three, 3), along_z(three[0:176], -3)]
    *xs, x_low, x_high = prepare(
        lambda x_ref, _, *refs: sample_kernel(x_ref, *refs), name="samples", in_specs=[VMEM, ANYWHERE]
    )(samples, three)
    column = join([three, *far], x_low)
    x_low = lax.ppermute(x_low, "rows", forward)
    x_high = lax.ppermute(x_high, "rows", backward)
    up, down = along_y(column, 1), along_y(column, -1)
    mean, var = fine_x(xs[0], x_low, x_high, column)
    far = [along_y(cut(up, 0, mean), 1), along_y(cut(down, 1, mean), -1)]
    coarse = coarse_x(xs, x_low, x_high, up, down)
    whole = jnp.concatenate([column, up, *far, down], axis=0)
    *ts, t_low, t_high = prepare(truth_kernel, name="truth", in_specs=[VMEM, ANYWHERE, ANYWHERE])(
        whole, mean, coarse[3]
    )
    t_low = lax.ppermute(t_low, "rows", forward)
    t_high = lax.ppermute(t_high, "rows", backward)
    fine = fine_t(xs[0], ts[0], mean, var)
    return coarse_t(xs, ts, (x_low, x_high, t_low, t_high), coarse, mean, var, fine)


def solution(mesh):
    placed = (P("samp", "rows", None), P("rows", "samp"))
    return jax.shard_map(
        local,
        mesh=mesh,
        in_specs=placed,
        out_specs=(P("samp", "rows", None),) * 5,
        check_vma=False,
    )
```

time: 99.9 us -> 71.6 us (0.72)
  waiting for transfers between devices: 24 us -> 10.2 us
  Pallas kernels: 35.3 us -> 23.6 us
  local copies, waits for them, and re-layouts: 7.89 us -> 1.47 us
  starting transfers between devices: 30.6 us -> 33.4 us
    pallas_call x3 -> x9, Pallas kernels: 33.7 us -> 22 us  [the longest x1 6.47 us: coarse_t(): pl.pallas_call(coarse_t_kernel, grid=(1,), out_shape=shapes, in_specs=[VM...]
    ppermute x7 -> x4, waiting for transfers between devices: 13.7 us -> 5.41 us  [along_z(): return lax.ppermute(x, 'samp', shifted(8, 4, k))]
    ppermute x1, starting transfers between devices: 1.92 us -> 6.34 us  [local(): x_high = lax.ppermute(x_high, 'rows', backward)]
    pallas_call x3 -> x0, local copies, waits for them, and re-layouts: 4.35 us -> none  [local(): pl.pallas_call(maps_kernel, out_shape=[jax.ShapeDtypeStruct((1, ROWS[k],...]
    ppermute x1, waiting for transfers between devices: 4.29 us -> 0.79 us  [local(): t_high = lax.ppermute(t_high, 'rows', backward)]
    ppermute x3 -> x4, waiting for transfers between devices: 4.05 us -> 1.68 us  [along_y(): return lax.ppermute(x, 'samp', shifted(4, 1, k))]
    ppermute x1, starting transfers between devices: 5.38 us -> 3.02 us  [local(): x_low = lax.ppermute(x_low, 'rows', forward)]
    ppermute x3 -> x4, starting transfers between devices: 4.6 us -> 6.92 us  [along_y(): return lax.ppermute(x, 'samp', shifted(4, 1, k))]
  transfers between devices with their start and end apart: 14 -> 12, of which waited for: 10 -> 8; matrix products, arithmetic and copies ran while one was open for 0% -> 1% of each run, Pallas kernels for 8% -> 19%
where the time goes in v2:
time: 71.6 us; the launch traced here: 71.2 us
  starting transfers between devices  33.4 us (47%)
  Pallas kernels  23.6 us (33%)
  waiting for transfers between devices  10.2 us (14%)
  other arithmetic  1.6 us (2%)
  local copies, waits for them, and re-layouts  1.47 us (2%)
  between operations  0.92 us (1%)
    ppermute x4, starting transfers between devices, along_z(): return lax.ppermute(x, 'samp', shifted(8, 4, k))  10.9 us
    ppermute x4, starting transfers between devices, along_y(): return lax.ppermute(x, 'samp', shifted(4, 1, k))  6.92 us
    pallas_call x1, Pallas kernels, coarse_t(): pl.pallas_call(coarse_t_kernel, grid=(1,), out_shape=shapes, in_specs=[VM...  6.47 us
    ppermute x1, starting transfers between devices, local(): x_high = lax.ppermute(x_high, 'rows', backward)  6.34 us
    pallas_call x1, Pallas kernels, fine_t(): pl.pallas_call(fine_t_kernel, grid=(STRIPS[0] // CHUNK,), out_shape=jax.S...  5.46 us
    ppermute x4, waiting for transfers between devices, along_z(): return lax.ppermute(x, 'samp', shifted(8, 4, k))  5.41 us
    ppermute x1, starting transfers between devices, local(): t_low = lax.ppermute(t_low, 'rows', forward)  4.2 us
    pallas_call x1, Pallas kernels, fine_x(): pl.pallas_call(lambda *refs: fine_x_kernel(*refs[0:6], *refs[6 + len(befo...  4 us
  transfers between devices with their start and end apart: 12, of which 8 were waited for; matrix products, arithmetic and copies ran while one was open for 1% of the time, Pallas kernels for 19%

profile of v2, /device:TPU:1, one launch (start us, length us, event | category | flops | bytes accessed | tf_op | source)
XLA Modules:
  0.0 71.2 jit_solution(13668647650548924345)
XLA Ops:
  0.6 1.7 %pack.1 = f32[88,128]{1,0:T(8,128)} custom-call(f32[140,80]{1,0:T(8,128)} %bitcast.4), custom_call_target="tpu_custom_call" | custom-call | tf_op jit(solution)/shard_map/pack/pallas_call | solution.py:593
  2.3 6.4 %collective-permute-start.1 = (f32[88,128]{1,0:T(8,128)}, f32[88,128]{1,0:T(8,128)S(1)}, u32[]{:S(2)}, u32[]{:S(2)}) collective-permute-start(f32[88,128]{1,0:T(8,128)} %pack.1), channel_id=1, source_target_pairs={{0,224},{8,232},{16,240},{24,248},{32,0},{40,8},{48,16},{56,24},{6... | collective-permute-start | bytes 135176 | tf_op jit(solution)/shard_map/ppermute | solution.py:431
  8.7 1.5 %collective-permute-done.1 = f32[88,128]{1,0:T(8,128)S(1)} collective-permute-done((f32[88,128]{1,0:T(8,128)}, f32[88,128]{1,0:T(8,128)S(1)}, u32[]{:S(2)}, u32[]{:S(2)}) %collective-permute-start.1) | collective-permute-done | bytes 45088 | tf_op jit(solution)/shard_map/ppermute | solution.py:431
  10.2 2.9 %collective-permute-done = f32[88,128]{1,0:T(8,128)S(1)} collective-permute-done((f32[88,128]{1,0:T(8,128)}, f32[88,128]{1,0:T(8,128)S(1)}, u32[]{:S(2)}, u32[]{:S(2)}) %collective-permute-start) | collective-permute-done | bytes 45088 | tf_op jit(solution)/shard_map/ppermute | solution.py:431
  14.7 4.5 %collective-permute-start.3 = (f32[176,128]{1,0:T(8,128)S(1)}, f32[176,128]{1,0:T(8,128)S(1)}, u32[]{:S(2)}, u32[]{:S(2)}) collective-permute-start(f32[176,128]{1,0:T(8,128)S(1)} %pad_maximum_fusion.1), channel_id=1, source_target_pairs={{0,160},{8,168},{16,176},{24,184},{32,192},{40,200},{48,208},{56,2... | collective-permute-start | bytes 270344 | tf_op jit(solution)/shard_map/ppermute | solution.py:431
  19.2 1.4 %copy-done = f32[1,80,4480]{2,1,0:T(8,128)S(1)} copy-done((f32[1,80,4480]{2,1,0:T(8,128)S(1)}, f32[1,80,4480]{2,1,0:T(8,128)}, u32[]{:S(2)}) %copy-start) | copy-done | bytes 1433624
  20.5 1.3 %samples.1 = (f32[36,80,128]{2,1,0:T(8,128)S(1)}, f32[19,48,128]{2,1,0:T(8,128)S(1)}, f32[10,32,128]{2,1,0:T(8,128)S(1)}, f32[6,16,128]{2,1,0:T(8,128)S(1)}, f32...) custom-call(f32[1,80,4480]{2,1,0:T(8,128)S(1)} %copy-done, ...), custom_call_target="tpu_custom_call" | custom-call | bytes 200000000 | tf_op jit(solution)/shard_map/samples/pallas_call | solution.py:602
  21.9 1.1 %collective-permute-done.3.refs_2_ = f32[176,128]{1,0:T(8,128)S(1)} collective-permute-done((f32[176,128]{1,0:T(8,128)S(1)}, f32[176,128]{1,0:T(8,128)S(1)}, u32[]{:S(2)}, u32[]{:S(2)}) %collective-permute-start.3) | collective-permute-done | bytes 90144 | tf_op jit(solution)/shard_map/ppermute | solution.py:431
  23.0 1.4 %collective-permute-start.4 = (f32[704,128]{1,0:T(8,128)S(1)}, f32[704,128]{1,0:T(8,128)S(1)}, u32[]{:S(2)}, u32[]{:S(2)}) collective-permute-start(f32[704,128]{1,0:T(8,128)S(1)} %join.1.refs_6_), channel_id=1, source_target_pairs={{0,8},{8,16},{16,24},{24,0},{32,40},{40,48},{48,56},{56,32},{64,72... | collective-permute-start | bytes 1081352 | tf_op jit(solution)/shard_map/ppermute | solution.py:435
  24.4 6.3 %collective-permute-start.6 = (f32[75,8,128]{2,1,0:T(8,128)S(1)}, f32[75,8,128]{2,1,0:T(8,128)S(1)}, u32[]{:S(2)}, u32[]{:S(2)}) collective-permute-start(f32[75,8,128]{2,1,0:T(8,128)S(1)} %get-tuple-element.40), channel_id=1, source_target_pairs={{1,0},{2,1},{3,2},{4,3},{5,4},{6,5},{7,6},{9,8},{10,9},{11,10},{12... | collective-permute-start | bytes 921608 | tf_op jit(solution)/shard_map/ppermute | solution.py:607
  30.7 3.0 %collective-permute-start.5 = (f32[75,8,128]{2,1,0:T(8,128)S(1)}, f32[75,8,128]{2,1,0:T(8,128)S(1)}, u32[]{:S(2)}, u32[]{:S(2)}) collective-permute-start(f32[75,8,128]{2,1,0:T(8,128)S(1)} %get-tuple-element.38.refs_3_), channel_id=1, source_target_pairs={{0,1},{1,2},{2,3},{3,4},{4,5},{5,6},{6,7},{8,9},{9,10},{10,11},{11... | collective-permute-start | bytes 921608 | tf_op jit(solution)/shard_map/ppermute | solution.py:606
  33.7 1.5 %collective-permute-start.8 = (f32[704,128]{1,0:T(8,128)S(1)}, f32[704,128]{1,0:T(8,128)S(1)}, u32[]{:S(2)}, u32[]{:S(2)}) collective-permute-start(f32[704,128]{1,0:T(8,128)S(1)} %join.1.refs_6_), channel_id=1, source_target_pairs={{0,24},{8,0},{16,8},{24,16},{32,56},{40,32},{48,40},{56,48},{64,88... | collective-permute-start | bytes 1081352 | tf_op jit(solution)/shard_map/ppermute | solution.py:435
  35.2 1.4 %collective-permute-done.6.refs_4_.refs_5_.refs_9_ = f32[75,8,128]{2,1,0:T(8,128)S(1)} collective-permute-done((f32[75,8,128]{2,1,0:T(8,128)S(1)}, f32[75,8,128]{2,1,0:T(8,128)S(1)}, u32[]{:S(2)}, u32[]{:S(2)}) %collective-permute-start.6) | collective-permute-done | bytes 307232 | tf_op jit(solution)/shard_map/ppermute | solution.py:607
  36.6 0.9 %collective-permute-done.5.refs_2_.refs_3_.refs_4_.refs_8_ = f32[75,8,128]{2,1,0:T(8,128)S(1)} collective-permute-done((f32[75,8,128]{2,1,0:T(8,128)S(1)}, f32[75,8,128]{2,1,0:T(8,128)S(1)}, u32[]{:S(2)}, u32[]{:S(2)}) %collective-permute-start.5) | collective-permute-done | bytes 307232 | tf_op jit(solution)/shard_map/ppermute | solution.py:606
  37.5 4.0 %fine_x.1 = (f32[36,80,128]{2,1,0:T(8,128)S(1)}, f32[36,80,128]{2,1,0:T(8,128)S(1)}) custom-call(f32[36,80,128]{2,1,0:T(8,128)S(1)} %get-tuple-element.39.refs_0_.refs_1_.x_ref.x_next.refs_20_.refs_21_, f32[36,80,128]{2,1,0:T(8,128)S(1)} %get-tuple-element.39.refs_0_.refs_1_.x_ref.x_next.refs_20_.refs_21_, ...), custom_call_target="tpu_custom_call" | custom-call | bytes 250000000 | tf_op jit(solution)/shard_map/fine_x/pallas_call | solution.py:491
  41.6 1.4 %collective-permute-start.7 = (f32[352,128]{1,0:T(8,128)S(1)}, f32[352,128]{1,0:T(8,128)S(1)}, u32[]{:S(2)}, u32[]{:S(2)}) collective-permute-start(f32[352,128]{1,0:T(8,128)S(1)} %cut.2), channel_id=1, source_target_pairs={{0,8},{8,16},{16,24},{24,0},{32,40},{40,48},{48,56},{56,32},{64,72... | collective-permute-start | bytes 540680 | tf_op jit(solution)/shard_map/ppermute | solution.py:435
  42.9 1.2 %collective-permute-done.8.ref.refs_7_ = f32[704,128]{1,0:T(8,128)S(1)} collective-permute-done((f32[704,128]{1,0:T(8,128)S(1)}, f32[704,128]{1,0:T(8,128)S(1)}, u32[]{:S(2)}, u32[]{:S(2)}) %collective-permute-start.8) | collective-permute-done | bytes 360480 | tf_op jit(solution)/shard_map/ppermute | solution.py:435
  44.1 2.7 %collective-permute-start.9 = (f32[352,128]{1,0:T(8,128)S(1)}, f32[352,128]{1,0:T(8,128)S(1)}, u32[]{:S(2)}, u32[]{:S(2)}) collective-permute-start(f32[352,128]{1,0:T(8,128)S(1)} %cut.3), channel_id=1, source_target_pairs={{0,24},{8,0},{16,8},{24,16},{32,56},{40,32},{48,40},{56,48},{64,88... | collective-permute-start | bytes 540680 | tf_op jit(solution)/shard_map/ppermute | solution.py:435
  46.9 3.0 %coarse_x.1 = (f32[18,48,128]{2,1,0:T(8,128)S(1)}, f32[9,32,128]{2,1,0:T(8,128)S(1)}, f32[5,16,128]{2,1,0:T(8,128)S(1)}, f32[3,16,128]{2,1,0:T(8,128)S(1)}, f32[...) custom-call(f32[19,48,128]{2,1,0:T(8,128)S(1)} %get-tuple-element.34., ...), custom_call_target="tpu_custom_call" | custom-call | bytes 250000000 | tf_op jit(solution)/shard_map/coarse_x/pallas_call | solution.py:511
  50.5 1.7 %truth.1 = (f32[36,80,128]{2,1,0:T(8,128)S(1)}, f32[19,48,128]{2,1,0:T(8,128)S(1)}, f32[10,32,128]{2,1,0:T(8,128)S(1)}, f32[6,16,128]{2,1,0:T(8,128)S(1)}, f32[4...) custom-call(f32[2816,128]{1,0:T(8,128)S(1)} %constant_dynamic-update-slice_fusion.g_ref, ...), custom_call_target="tpu_custom_call" | custom-call | bytes 200000000 | tf_op jit(solution)/shard_map/truth/pallas_call | solution.py:613
  52.2 4.2 %collective-permute-start.10 = (f32[75,8,128]{2,1,0:T(8,128)S(1)}, f32[75,8,128]{2,1,0:T(8,128)S(1)}, u32[]{:S(2)}, u32[]{:S(2)}) collective-permute-start(f32[75,8,128]{2,1,0:T(8,128)S(1)} %get-tuple-element.47), channel_id=1, source_target_pairs={{0,1},{1,2},{2,3},{3,4},{4,5},{5,6},{6,7},{8,9},{9,10},{10,11},{11... | collective-permute-start | bytes 921608 | tf_op jit(solution)/shard_map/ppermute | solution.py:616
  56.4 1.9 %collective-permute-start.11 = (f32[75,8,128]{2,1,0:T(8,128)S(1)}, f32[75,8,128]{2,1,0:T(8,128)S(1)}, u32[]{:S(2)}, u32[]{:S(2)}) collective-permute-start(f32[75,8,128]{2,1,0:T(8,128)S(1)} %get-tuple-element.48), channel_id=1, source_target_pairs={{1,0},{2,1},{3,2},{4,3},{5,4},{6,5},{7,6},{9,8},{10,9},{11,10},{12... | collective-permute-start | bytes 921608 | tf_op jit(solution)/shard_map/ppermute | solution.py:617
  58.3 5.5 %fine_t.1.refs_28_ = f32[1,80,4480]{2,1,0:T(8,128)} custom-call(f32[36,80,128]{2,1,0:T(8,128)S(1)} %get-tuple-element.39.refs_0_.refs_1_.x_ref.x_next.refs_20_.refs_21_, f32[36,80,128]{2,1,0:T(8,128)S(1)} %get-tuple-element.39.refs_0_.refs_1_.x_ref.x_next.refs_20_.refs_21_, f32[36,80,128]{2,1,0:T(8,128)S(1)} %get-tuple-element.56.t_ref.t_next.refs_22_.refs_23_, ...), custom_call_target="tpu_custom_call" | custom-call | bytes 400000000 | tf_op jit(solution)/shard_map/fine_t/pallas_call | solution.py:531
  64.6 6.5 %coarse_t.1 = (f32[1,80,4480]{2,1,0:T(8,128)}, f32[1,40,2240]{2,1,0:T(8,128)}, f32[20,1,1120]{2,1,0:T(1,128)}, f32[10,1,560]{2,1,0:T(1,128)}, f32[5,1,280]{2,1,0:T(1,128)}) custom-call(f32[19,48,128]{2,1,0:T(8,128)S(1)} %get-tuple-element.34.refs_0_, f32[10,32,128]{2,1,0:T(8,128)S(1)} %get-tuple-element.35.refs_1_, ...), custom_call_target="tpu_custom_call", output_to_operand_aliasing={{0}: (28, {})} | custom-call | tf_op jit(solution)/shard_map/coarse_t/pallas_call | solution.py:558
  (19 shorter events, 3.1 us)
Async XLA Ops:
  2.3 7.9 %collective-permute-start.1 = (f32[88,128]{1,0:T(8,128)}, f32[88,128]{1,0:T(8,128)S(1)}, u32[]{:S(2)}, u32[]{:S(2)}) collective-permute-start(f32[88,128]{1,0:T(8,128)} %pack.1), channel_id=1, source_target_pairs={{0,224},{8,232},{16,240},{24,248},{32,0},{40,8},{48,16},{56,24},{6... | collective-permute-start | bytes 135176 | tf_op jit(solution)/shard_map/ppermute | solution.py:431
  8.7 4.3 %collective-permute-start = (f32[88,128]{1,0:T(8,128)}, f32[88,128]{1,0:T(8,128)S(1)}, u32[]{:S(2)}, u32[]{:S(2)}) collective-permute-start(f32[88,128]{1,0:T(8,128)} %pack.1), channel_id=1, source_target_pairs={{0,32},{8,40},{16,48},{24,56},{32,64},{40,72},{48,80},{56,88},{64,... | collective-permute-start | bytes 135176 | tf_op jit(solution)/shard_map/ppermute | solution.py:431
  13.8 9.1 %collective-permute-start.2 = (f32[264,128]{1,0:T(8,128)S(1)}, f32[264,128]{1,0:T(8,128)S(1)}, u32[]{:S(2)}, u32[]{:S(2)}) collective-permute-start(f32[264,128]{1,0:T(8,128)S(1)} %pad_maximum_fusion._.refs_0_), channel_id=1, source_target_pairs={{0,96},{8,104},{16,112},{24,120},{32,128},{40,136},{48,144},{56,15... | collective-permute-start | bytes 405512 | tf_op jit(solution)/shard_map/ppermute | solution.py:431
  14.7 8.3 %collective-permute-start.3 = (f32[176,128]{1,0:T(8,128)S(1)}, f32[176,128]{1,0:T(8,128)S(1)}, u32[]{:S(2)}, u32[]{:S(2)}) collective-permute-start(f32[176,128]{1,0:T(8,128)S(1)} %pad_maximum_fusion.1), channel_id=1, source_target_pairs={{0,160},{8,168},{16,176},{24,184},{32,192},{40,200},{48,208},{56,2... | collective-permute-start | bytes 270344 | tf_op jit(solution)/shard_map/ppermute | solution.py:431
  19.2 1.4 %copy-start = (f32[1,80,4480]{2,1,0:T(8,128)S(1)}, f32[1,80,4480]{2,1,0:T(8,128)}, u32[]{:S(2)}) copy-start(f32[1,80,4480]{2,1,0:T(8,128)} %x_ref.1) | copy-start | bytes 4300804
  23.0 18.5 %collective-permute-start.4 = (f32[704,128]{1,0:T(8,128)S(1)}, f32[704,128]{1,0:T(8,128)S(1)}, u32[]{:S(2)}, u32[]{:S(2)}) collective-permute-start(f32[704,128]{1,0:T(8,128)S(1)} %join.1.refs_6_), channel_id=1, source_target_pairs={{0,8},{8,16},{16,24},{24,0},{32,40},{40,48},{48,56},{56,32},{64,72... | collective-permute-start | bytes 1081352 | tf_op jit(solution)/shard_map/ppermute | solution.py:435
  24.4 12.3 %collective-permute-start.6 = (f32[75,8,128]{2,1,0:T(8,128)S(1)}, f32[75,8,128]{2,1,0:T(8,128)S(1)}, u32[]{:S(2)}, u32[]{:S(2)}) collective-permute-start(f32[75,8,128]{2,1,0:T(8,128)S(1)} %get-tuple-element.40), channel_id=1, source_target_pairs={{1,0},{2,1},{3,2},{4,3},{5,4},{6,5},{7,6},{9,8},{10,9},{11,10},{12... | collective-permute-start | bytes 921608 | tf_op jit(solution)/shard_map/ppermute | solution.py:607
  30.7 6.8 %collective-permute-start.5 = (f32[75,8,128]{2,1,0:T(8,128)S(1)}, f32[75,8,128]{2,1,0:T(8,128)S(1)}, u32[]{:S(2)}, u32[]{:S(2)}) collective-permute-start(f32[75,8,128]{2,1,0:T(8,128)S(1)} %get-tuple-element.38.refs_3_), channel_id=1, source_target_pairs={{0,1},{1,2},{2,3},{3,4},{4,5},{5,6},{6,7},{8,9},{9,10},{10,11},{11... | collective-permute-start | bytes 921608 | tf_op jit(solution)/shard_map/ppermute | solution.py:606
  33.7 10.4 %collective-permute-start.8 = (f32[704,128]{1,0:T(8,128)S(1)}, f32[704,128]{1,0:T(8,128)S(1)}, u32[]{:S(2)}, u32[]{:S(2)}) collective-permute-start(f32[704,128]{1,0:T(8,128)S(1)} %join.1.refs_6_), channel_id=1, source_target_pairs={{0,24},{8,0},{16,8},{24,16},{32,56},{40,32},{48,40},{56,48},{64,88... | collective-permute-start | bytes 1081352 | tf_op jit(solution)/shard_map/ppermute | solution.py:435
  41.6 8.3 %collective-permute-start.7 = (f32[352,128]{1,0:T(8,128)S(1)}, f32[352,128]{1,0:T(8,128)S(1)}, u32[]{:S(2)}, u32[]{:S(2)}) collective-permute-start(f32[352,128]{1,0:T(8,128)S(1)} %cut.2), channel_id=1, source_target_pairs={{0,8},{8,16},{16,24},{24,0},{32,40},{40,48},{48,56},{56,32},{64,72... | collective-permute-start | bytes 540680 | tf_op jit(solution)/shard_map/ppermute | solution.py:435
  44.1 6.3 %collective-permute-start.9 = (f32[352,128]{1,0:T(8,128)S(1)}, f32[352,128]{1,0:T(8,128)S(1)}, u32[]{:S(2)}, u32[]{:S(2)}) collective-permute-start(f32[352,128]{1,0:T(8,128)S(1)} %cut.3), channel_id=1, source_target_pairs={{0,24},{8,0},{16,8},{24,16},{32,56},{40,32},{48,40},{56,48},{64,88... | collective-permute-start | bytes 540680 | tf_op jit(solution)/shard_map/ppermute | solution.py:435
  52.2 11.6 %collective-permute-start.10 = (f32[75,8,128]{2,1,0:T(8,128)S(1)}, f32[75,8,128]{2,1,0:T(8,128)S(1)}, u32[]{:S(2)}, u32[]{:S(2)}) collective-permute-start(f32[75,8,128]{2,1,0:T(8,128)S(1)} %get-tuple-element.47), channel_id=1, source_target_pairs={{0,1},{1,2},{2,3},{3,4},{4,5},{5,6},{6,7},{8,9},{9,10},{10,11},{11... | collective-permute-start | bytes 921608 | tf_op jit(solution)/shard_map/ppermute | solution.py:616
  56.4 8.2 %collective-permute-start.11 = (f32[75,8,128]{2,1,0:T(8,128)S(1)}, f32[75,8,128]{2,1,0:T(8,128)S(1)}, u32[]{:S(2)}, u32[]{:S(2)}) collective-permute-start(f32[75,8,128]{2,1,0:T(8,128)S(1)} %get-tuple-element.48), channel_id=1, source_target_pairs={{1,0},{2,1},{3,2},{4,3},{5,4},{6,5},{7,6},{9,8},{10,9},{11,10},{12... | collective-permute-start | bytes 921608 | tf_op jit(solution)/shard_map/ppermute | solution.py:617

commit v3 on v2

v3 whole, which is shorter than its diff:
```python
import functools

import jax
import jax.numpy as jnp
import numpy as np
from jax import lax
from jax.experimental import pallas as pl
from jax.experimental.pallas import tpu as pltpu
from jax.sharding import PartitionSpec as P

small_one = 0.0001
small_two = 0.0009

ROWS = (80, 40, 20, 10, 5)
COLS = (4480, 2240, 1120, 560, 280)
TILES = tuple(-(-c // 128) for c in COLS)
STRIPS = tuple(t + 1 for t in TILES)
HELD = (80, 48, 32, 16, 8)
POOLED = (80, 40, 24, 16, 8)
WORK = (80, 48, 32, 16, 16)
EDGE_AT = tuple(int(v) for v in np.cumsum((0,) + STRIPS))
EDGES = EDGE_AT[-1]
ORDER = (0, 1, 7, 3, 4, 2, 5, 6)
GROUP = 9
CHUNK = 9
f32, bf16 = jnp.float32, jnp.bfloat16
VMEM = pl.BlockSpec(memory_space=pltpu.VMEM)
ANYWHERE = pl.BlockSpec(memory_space=pl.ANY)
PARAMS = pltpu.CompilerParams(vmem_limit_bytes=20 * 1024 * 1024)


def window():
    offsets = np.arange(11).astype(np.float32) - np.float32(5.0)
    shaped = np.exp(-offsets * offsets / np.float32(4.5))
    return (shaped / shaped.sum(dtype=np.float32)).astype(np.float32)


TAPS = [float(v) for v in window()]


def split(value):
    high = value.astype(bf16)
    return high, (value - high.astype(f32)).astype(bf16)


def column_band():
    row = lax.broadcasted_iota(jnp.int32, (256, 128), 0)
    col = lax.broadcasted_iota(jnp.int32, (256, 128), 1)
    band = jnp.zeros((256, 128), f32)
    for tap in range(11):
        band = jnp.where(row - col == 59 + tap, TAPS[tap], band)
    return band


def pair_matrix():
    row = lax.broadcasted_iota(jnp.int32, (256, 128), 0)
    col = lax.broadcasted_iota(jnp.int32, (256, 128), 1)
    lane = jnp.where(row >= 128, row - 128, row)
    half = lane // 2
    side = jnp.where(lane >= 64, half - 32, half + 96)
    goal = jnp.where(row < 128, half + 32, side)
    return jnp.where(goal == col, 0.25, 0.0).astype(bf16)


def lanes(rows):
    return lax.broadcasted_iota(jnp.int32, (rows, 128), 1)


def pyramid(levels, low_ref, high_ref, pair_ref):
    pair_ref[...] = pair_matrix()
    for k in range(1, 5):
        src, dst = levels[k - 1], levels[k]
        rows = POOLED[k]
        pairs = pair_ref[...]
        lower = lanes(rows) < 64

        def rowsum(u):
            return src[u, pl.ds(0, rows, stride=2), :] + src[u, pl.ds(1, rows, stride=2), :]

        count = STRIPS[k - 1]
        for s in range(STRIPS[k]):
            zero = jnp.zeros((rows, 128), f32)
            middle = rowsum(2 * s) if 2 * s < count else zero
            left = rowsum(2 * s - 1) if 0 <= 2 * s - 1 < count else zero
            right = rowsum(2 * s + 1) if 2 * s + 1 < count else zero
            both = jnp.concatenate([middle, jnp.where(lower, right, left)], axis=1)
            first = both.astype(bf16)
            rest = both - first.astype(f32)
            second, third = split(rest)
            total = jnp.dot(third, pairs, preferred_element_type=f32)
            total += jnp.dot(second, pairs, preferred_element_type=f32)
            total += jnp.dot(first, pairs, preferred_element_type=f32)
            dst[s, 0:rows] = total
    for k in range(5):
        at, n, rows = EDGE_AT[k], STRIPS[k], ROWS[k]
        high_ref[at : at + n] = levels[k][:, 0:8, :]
        if rows >= 8:
            low_ref[at : at + n] = levels[k][:, rows - 8 : rows, :]
        else:
            low_ref[at : at + n, 0 : 8 - rows] = jnp.zeros((n, 8 - rows, 128), f32)
            low_ref[at : at + n, 8 - rows : 8] = levels[k][:, 0:rows, :]


def sample_kernel(x_ref, *refs):
    levels, low_ref, high_ref, pair_ref = refs[0:5], refs[5], refs[6], refs[7]
    lower = lanes(80) < 64
    before = jnp.zeros((80, 128), f32)
    for s in range(STRIPS[0]):
        now = jnp.zeros((80, 128), f32)
        if s < TILES[0]:
            now = pltpu.roll(x_ref[0, :, 128 * s : 128 * s + 128], 64, 1)
        levels[0][s] = jnp.where(lower, before, now)
        before = now
    pyramid(levels, low_ref, high_ref, pair_ref)


def pack_kernel(t_ref, out_ref):
    out_ref[0:80] = t_ref[0:128, :].T
    rest = t_ref[128:140, :].T
    parts = [rest[8 * a : 8 * a + 8] for a in range(10)]
    out_ref[80:88] = jnp.concatenate(parts + [jnp.zeros((8, 8), f32)], axis=1)


def truth_kernel(g_ref, *refs):
    refs = refs[1:]
    levels, low_ref, high_ref, pair_ref = refs[0:5], refs[5], refs[6], refs[7]
    me = lax.axis_index("samp")
    my_z, my_y = me // 4, me % 4
    held = {}
    lane = lanes(80)
    for s in range(32):
        dz = lax.rem(my_z - s // 4 + 8, 8)
        slot = dz
        for apart in (2, 5, 6, 7):
            slot = jnp.where(dz == apart, ORDER.index(apart), slot)
        dy = lax.rem(my_y - s % 4 + 4, 4)
        at = pl.multiple_of((dy * 8 + slot) * 88, 8)
        start = 64 + 140 * s
        q, off = start // 128, start % 128
        main = pltpu.roll(g_ref[pl.ds(at, 80), :], off, 1)
        tail8 = g_ref[pl.ds(pl.multiple_of(at + 80, 8), 8), :]
        tail = jnp.concatenate([pltpu.roll(tail8, (off - 12 * a) % 128, 1) for a in range(10)], axis=0)
        held.setdefault(q, []).append((main, off, 128))
        held.setdefault(q + 1, []).append((main, 0, off))
        held.setdefault(q + 1, []).append((tail, off, min(128, off + 12)))
        if off + 12 > 128:
            held.setdefault(q + 2, []).append((tail, 0, off + 12 - 128))
        last = 35 if s == 31 else (64 + 140 * (s + 1)) // 128 - 1
        for tile in sorted(held):
            if tile <= last:
                value = jnp.zeros((80, 128), f32)
                for piece, lo, hi in held.pop(tile):
                    if hi > lo:
                        value = jnp.where((lane >= lo) & (lane < hi), piece, value)
                levels[0][tile] = value
    pyramid(levels, low_ref, high_ref, pair_ref)


def set_bands(band_ref, third_ref=None):
    band = column_band()
    high, low = split(band)
    band_ref[:, 0:128] = high
    band_ref[:, 128:256] = low
    if third_ref is not None:
        third_ref[...] = ((band - high.astype(f32)) - low.astype(f32)).astype(bf16)


def row_sum(read, work):
    total = TAPS[5] * read(5, work)
    for tap in range(5):
        total = total + TAPS[tap] * (read(tap, work) + read(10 - tap, work))
    return total


def keep(at, slot, parts, total):
    n = total.shape[0]
    for p, ref in enumerate(parts):
        part = total.astype(bf16)
        ref[slot, at : at + n] = part
        if p + 1 < len(parts):
            total = total - part.astype(f32)


def column_sum(j, count, n, parts, band_ref, third_ref=None):
    def pairs(ref):
        return jnp.concatenate(
            [
                ref[j : j + count, 0:n].reshape(count * n, 128),
                ref[j + 1 : j + count + 1, 0:n].reshape(count * n, 128),
            ],
            axis=1,
        )

    acc = None
    for ref in reversed(parts):
        one = jnp.dot(pairs(ref), band_ref[...], preferred_element_type=f32)
        acc = one if acc is None else acc + one
    acc = acc[:, 0:128] + acc[:, 128:256]
    if third_ref is not None:
        acc = jnp.dot(pairs(parts[0]), third_ref[...], preferred_element_type=f32) + acc
    return acc


def ratio(mean_x, var_x, mean_y, second_y, cross, coarsest=False):
    square_y, product = mean_y * mean_y, mean_x * mean_y
    result = (2.0 * (cross - product) + small_two) / (
        var_x + (second_y - square_y) + small_two
    )
    if coarsest:
        result = (2.0 * product + small_one) / (mean_x * mean_x + square_y + small_one) * result
    return result


def fine_x_kernel(x_ref, x_next, mean_ref, var_ref, *scratch):
    band_ref, fields, v_high, v_low = scratch

    def vertical(x, slot):
        at = slot % 3
        value = x[...]
        fields[at] = value * value
        keep(0, slot, (v_high, v_low), row_sum(lambda i, n: x[3 + i : 3 + i + n], 64))
        total = row_sum(lambda i, n: fields[at, 3 + i : 3 + i + n], 64)
        keep(64, slot, (v_high, v_low), total)

    def finish(j):
        acc = column_sum(j, GROUP, 128, (v_high, v_low), band_ref)
        for g in range(GROUP):
            mean = acc[128 * g : 128 * g + 64]
            mean_ref[j + g] = mean
            var_ref[j + g] = acc[128 * g + 64 : 128 * g + 128] - mean * mean

    @pl.when(pl.program_id(0) == 0)
    def _():
        set_bands(band_ref)
        vertical(x_ref.at[0], 0)

    @pl.when(pl.program_id(0) > 0)
    def _():
        v_high[0] = v_high[CHUNK]
        v_low[0] = v_low[CHUNK]

    for j in range(CHUNK - 1):
        vertical(x_ref.at[j + 1], j + 1)
        if (j + 1) % GROUP == 0:
            finish(j + 1 - GROUP)
    vertical(x_next.at[0], CHUNK)
    finish(CHUNK - GROUP)


def fine_t_kernel(x_ref, x_next, t_ref, t_next, mean_ref, var_ref, out_ref, *scratch):
    band_ref, fields, v_high, v_low = scratch

    def vertical(x, t, slot):
        at = 2 * (slot % 3)
        tv = t[...]
        fields[at] = tv * tv
        fields[at + 1] = x[...] * tv
        keep(0, slot, (v_high, v_low), row_sum(lambda i, n: t[3 + i : 3 + i + n], 64))
        for f in range(2):
            total = row_sum(lambda i, n: fields[at + f, 3 + i : 3 + i + n], 64)
            keep(64 * f + 64, slot, (v_high, v_low), total)

    def finish(first):
        acc = column_sum(first, GROUP, 192, (v_high, v_low), band_ref)
        for g in range(GROUP):
            j, at = first + g, 192 * g
            out_ref[0, 8:72, j * 128 : j * 128 + 128] = ratio(
                mean_ref[j],
                var_ref[j],
                acc[at : at + 64],
                acc[at + 64 : at + 128],
                acc[at + 128 : at + 192],
            )

    @pl.when(pl.program_id(0) == 0)
    def _():
        set_bands(band_ref)
        vertical(x_ref.at[0], t_ref.at[0], 0)

    @pl.when(pl.program_id(0) > 0)
    def _():
        v_high[0] = v_high[CHUNK]
        v_low[0] = v_low[CHUNK]

    for j in range(CHUNK - 1):
        vertical(x_ref.at[j + 1], t_ref.at[j + 1], j + 1)
        if (j + 1) % GROUP == 0:
            finish(j + 1 - GROUP)
    vertical(x_next.at[0], t_next.at[0], CHUNK)
    finish(CHUNK - GROUP)


def groups(count, most):
    return [(first, min(most, count - first)) for first in range(0, count, most)]


def rest_x_kernel(*refs):
    xs, (low, high), x_ends = refs[0:4], refs[4:6], refs[6:8]
    means, variances = refs[8:13], refs[13:18]
    band_ref, third_ref, fields = refs[18:21]
    v_parts = refs[21:24]
    set_bands(band_ref, third_ref)

    def rows_of(f, start):
        return lambda i, n: fields[f, start + 3 + i : start + 3 + i + n]

    def store(k, first, count, work, acc):
        for g in range(count):
            row = 2 * work * g
            mean = acc[row : row + work]
            means[k][first + g] = mean
            variances[k][first + g] = acc[row + work : row + 2 * work] - mean * mean

    for s in range(STRIPS[0]):
        at = 2 * (s % 3)
        fields[at, 0:8] = low[s]
        fields[at, 8:24] = x_ends[0][s]
        fields[at, 24:40] = x_ends[1][s]
        fields[at, 40:48] = high[s]
        x = fields[at, 0:48]
        fields[at + 1, 0:48] = x * x
        for f in range(2):
            top = row_sum(rows_of(at + f, 0), 8)
            bottom = row_sum(rows_of(at + f, 24), 8)
            keep(16 * f, s, v_parts[0:2], jnp.concatenate([top, bottom], axis=0))
    for first, count in groups(TILES[0], 9):
        store(0, first, count, 16, column_sum(first, count, 32, v_parts[0:2], band_ref))
    for k in range(1, 5):
        rows, work, held = ROWS[k], WORK[k], HELD[k]
        parts, third = (v_parts, third_ref) if k >= 2 else (v_parts[0:2], None)
        for s in range(STRIPS[k]):
            at, edge = 2 * (s % 3), EDGE_AT[k] + s
            fields[at, 0:8] = low[edge]
            fields[at, 8 : 8 + held] = xs[k - 1][s]
            fields[at, 8 + rows : 16 + rows] = high[edge]
            x = fields[at, 0 : work + 16]
            fields[at + 1, 0 : work + 16] = x * x
            for f in range(2):
                keep(f * work, s, parts, row_sum(rows_of(at + f, 0), work))
        for first, count in groups(TILES[k], 9):
            acc = column_sum(first, count, 2 * work, parts, band_ref, third)
            store(k, first, count, work, acc)


def rest_kernel(*refs):
    xs, ts = refs[0:4], refs[4:8]
    x_low, x_high, t_low, t_high = refs[8:12]
    means, variances = refs[12:17], refs[17:22]
    x_ends, t_ends = refs[22:24], refs[24:26]
    out_fine, outs = refs[27], refs[28:32]
    band_ref, third_ref, fields = refs[32:35]
    v_parts, ends, sems = refs[35:38], refs[38], refs[39]
    set_bands(band_ref, third_ref)

    def rows_of(f, start):
        return lambda i, n: fields[f, start + 3 + i : start + 3 + i + n]

    def products(at, span):
        t, x = fields[at, 0:span], fields[at + 1, 0:span]
        fields[at + 1, 0:span] = t * t
        fields[at + 2, 0:span] = x * t

    for s in range(STRIPS[0]):
        at = 3 * (s % 3)
        for f, (two, low, high) in enumerate(((t_ends, t_low, t_high), (x_ends, x_low, x_high))):
            fields[at + f, 0:8] = low[s]
            fields[at + f, 8:24] = two[0][s]
            fields[at + f, 24:40] = two[1][s]
            fields[at + f, 40:48] = high[s]
        products(at, 48)
        for f in range(3):
            top = row_sum(rows_of(at + f, 0), 8)
            bottom = row_sum(rows_of(at + f, 24), 8)
            keep(16 * f, s, v_parts[0:2], jnp.concatenate([top, bottom], axis=0))
    for first, count in groups(TILES[0], 9):
        acc = column_sum(first, count, 48, v_parts[0:2], band_ref)
        for g in range(count):
            for end in range(2):
                j, row, side = first + g, 48 * g + 8 * end, slice(8 * end, 8 * end + 8)
                ends[end, :, 128 * j : 128 * j + 128] = ratio(
                    means[0][j, side],
                    variances[0][j, side],
                    acc[row : row + 8],
                    acc[row + 16 : row + 24],
                    acc[row + 32 : row + 40],
                )

    copies = [
        pltpu.make_async_copy(ends.at[end], out_fine.at[0, pl.ds(72 * end, 8), :], sems.at[end])
        for end in range(2)
    ]
    for copy in copies:
        copy.start()

    for k in range(1, 5):
        rows, work, held = ROWS[k], WORK[k], HELD[k]
        parts, third = (v_parts, third_ref) if k >= 2 else (v_parts[0:2], None)
        for s in range(STRIPS[k]):
            at, edge = 3 * (s % 3), EDGE_AT[k] + s
            for f, (ref, low, high) in enumerate(
                ((ts[k - 1], t_low, t_high), (xs[k - 1], x_low, x_high))
            ):
                fields[at + f, 0:8] = low[edge]
                fields[at + f, 8 : 8 + held] = ref[s]
                fields[at + f, 8 + rows : 16 + rows] = high[edge]
            products(at, work + 16)
            for f in range(3):
                keep(f * work, s, parts, row_sum(rows_of(at + f, 0), work))
        for first, count in groups(TILES[k], 9):
            acc = column_sum(first, count, 3 * work, parts, band_ref, third)
            for g in range(count):
                j, row, col = first + g, 3 * work * g, 128 * (first + g)
                three = (acc[row + f * work : row + f * work + rows] for f in range(3))
                map_ = ratio(means[k][j, 0:rows], variances[k][j, 0:rows], *three, k == 4)
                width = min(128, COLS[k] - col)
                if k == 1:
                    outs[0][0, :, col : col + width] = map_[:, 0:width]
                else:
                    outs[k - 1][:, 0, col : col + width] = map_[:, 0:width]

    for copy in copies:
        copy.wait()


def level_shapes():
    return [jax.ShapeDtypeStruct((STRIPS[k], HELD[k], 128), f32) for k in range(5)] + [
        jax.ShapeDtypeStruct((EDGES, 8, 128), f32)
    ] * 2


def shifted(n, stride, k):
    perm = []
    for i in range(32):
        c = (i // stride) % n
        perm.append((i, i + ((c + k) % n - c) * stride))
    return perm


def along_z(x, k):
    return lax.ppermute(x, "samp", shifted(8, 4, k))


def along_y(x, k):
    return lax.ppermute(x, "samp", shifted(4, 1, k))


def join_kernel(parts, outs):
    at = 0
    for part in parts:
        for out in outs:
            n = min(part.shape[0], out.shape[0] - at)
            if n > 0:
                out[at : at + n] = part[0:n]
        at += part.shape[0]


def join(parts, *before, head=None):
    rows, n = sum(part.shape[0] for part in parts), len(parts)
    sizes = [rows] if head is None else [rows, head]
    return pl.pallas_call(
        lambda *refs: join_kernel(refs[:n], refs[n + len(before) :]),
        out_shape=[jax.ShapeDtypeStruct((size, 128), f32) for size in sizes],
        in_specs=[VMEM] * n + [ANYWHERE] * len(before),
        out_specs=[VMEM] * len(sizes),
        compiler_params=PARAMS,
        cost_estimate=cost(0.02),
        name="join",
    )(*parts, *before)


def cut_kernel(up_ref, down_ref, first_ref, second_ref):
    n = first_ref.shape[0]
    first_ref[...] = up_ref[0:n]
    second_ref[...] = down_ref[n:]


def cut(up, down):
    n = up.shape[0] // 2
    return pl.pallas_call(
        cut_kernel,
        out_shape=[jax.ShapeDtypeStruct((n, 128), f32)] * 2,
        in_specs=[VMEM, VMEM],
        out_specs=[VMEM, VMEM],
        compiler_params=PARAMS,
        cost_estimate=cost(0.02),
        name="cut",
    )(up, down)


def chunk_spec(rows, base, step=None):
    if step is None:
        return pl.BlockSpec((CHUNK, rows, 128), lambda g: (g + base, 0, 0))
    return pl.BlockSpec(
        (1, rows, 128), lambda g: (jnp.minimum((g + base + 1) * CHUNK, STRIPS[0] - 1), 0, 0)
    )


def both_specs(rows, base):
    return [chunk_spec(rows, base), chunk_spec(rows, base, 1)]


def cost(micros):
    return pl.CostEstimate(flops=0, bytes_accessed=int(micros * 5e7), transcendentals=0)


def fine_x(x):
    return pl.pallas_call(
        fine_x_kernel,
        grid=(STRIPS[0] // CHUNK,),
        out_shape=[jax.ShapeDtypeStruct((STRIPS[0], 64, 128), f32)] * 2,
        in_specs=both_specs(80, 0),
        out_specs=[chunk_spec(64, 0)] * 2,
        scratch_shapes=[
            pltpu.VMEM((256, 256), bf16),
            pltpu.VMEM((3, 80, 128), f32),
            pltpu.VMEM((CHUNK + 1, 128, 128), bf16),
            pltpu.VMEM((CHUNK + 1, 128, 128), bf16),
        ],
        compiler_params=PARAMS,
        cost_estimate=cost(5),
        name="fine_x",
    )(x, x)


def fine_t(x, t, mean, var):
    return pl.pallas_call(
        fine_t_kernel,
        grid=(STRIPS[0] // CHUNK,),
        out_shape=jax.ShapeDtypeStruct((1, 80, COLS[0]), f32),
        in_specs=both_specs(80, 0) + both_specs(80, 0) + [chunk_spec(64, 0)] * 2,
        out_specs=pl.BlockSpec((1, 80, 128 * CHUNK), lambda g: (0, 0, g)),
        scratch_shapes=[
            pltpu.VMEM((256, 256), bf16),
            pltpu.VMEM((6, 80, 128), f32),
            pltpu.VMEM((CHUNK + 1, 192, 128), bf16),
            pltpu.VMEM((CHUNK + 1, 192, 128), bf16),
        ],
        compiler_params=PARAMS,
        cost_estimate=cost(8),
        name="fine_t",
    )(x, x, t, t, mean, var)


def ends(rows, last):
    return [
        pl.BlockSpec((STRIPS[0], rows, 128), lambda g: (0, 0, 0)),
        pl.BlockSpec((STRIPS[0], rows, 128), lambda g: (0, last, 0)),
    ]


def rest_x(xs, low, high):
    shapes = [jax.ShapeDtypeStruct((TILES[k], WORK[k] if k else 16, 128), f32) for k in range(5)]
    out = pl.pallas_call(
        rest_x_kernel,
        grid=(1,),
        out_shape=shapes * 2,
        in_specs=[VMEM] * 6 + ends(16, 4),
        out_specs=[VMEM] * 10,
        scratch_shapes=[
            pltpu.VMEM((256, 256), bf16),
            pltpu.VMEM((256, 128), bf16),
            pltpu.VMEM((6, 64, 128), f32),
            pltpu.VMEM((36, 96, 128), bf16),
            pltpu.VMEM((36, 96, 128), bf16),
            pltpu.VMEM((10, 64, 128), bf16),
        ],
        compiler_params=PARAMS,
        cost_estimate=cost(5),
        name="rest_x",
    )(*xs[1:], low, high, xs[0], xs[0])
    return out


def rest(xs, ts, edges, stats, fine):
    shapes = [jax.ShapeDtypeStruct((1, 80, COLS[0]), f32), jax.ShapeDtypeStruct((1, 40, COLS[1]), f32)]
    shapes += [jax.ShapeDtypeStruct((ROWS[k], 1, COLS[k]), f32) for k in range(2, 5)]
    fine, half, *small = pl.pallas_call(
        rest_kernel,
        grid=(1,),
        out_shape=shapes,
        in_specs=[VMEM] * 22 + ends(16, 4) * 2 + [ANYWHERE],
        out_specs=[ANYWHERE] + [VMEM] * 4,
        input_output_aliases={26: 0},
        scratch_shapes=[
            pltpu.VMEM((256, 256), bf16),
            pltpu.VMEM((256, 128), bf16),
            pltpu.VMEM((9, 64, 128), f32),
            pltpu.VMEM((36, 144, 128), bf16),
            pltpu.VMEM((36, 144, 128), bf16),
            pltpu.VMEM((10, 96, 128), bf16),
            pltpu.VMEM((2, 8, COLS[0]), f32),
            pltpu.SemaphoreType.DMA((2,)),
        ],
        compiler_params=pltpu.CompilerParams(vmem_limit_bytes=24 * 1024 * 1024),
        name="rest",
    )(*xs[1:], *ts[1:], *edges, *stats, xs[0], xs[0], ts[0], ts[0], fine)
    return (fine, half) + tuple(value.transpose(1, 0, 2) for value in small)


def local(samples, truth_field):
    forward = [(i, i + 1) for i in range(7)]
    backward = [(i + 1, i) for i in range(7)]
    prepare = functools.partial(
        pl.pallas_call,
        out_shape=level_shapes(),
        in_specs=[VMEM],
        out_specs=[VMEM] * 7,
        scratch_shapes=[pltpu.VMEM((256, 128), bf16)],
        compiler_params=PARAMS,
        cost_estimate=cost(4),
    )
    packed = pl.pallas_call(
        pack_kernel,
        out_shape=jax.ShapeDtypeStruct((88, 128), f32),
        in_specs=[VMEM],
        out_specs=VMEM,
        compiler_params=PARAMS,
        name="pack",
    )(truth_field.T)
    near = along_z(packed, 1)
    three, two = join([packed, near, along_z(packed, -1)], head=176)
    far = [along_z(three, 3), along_z(two, -3)]
    *xs, x_low, x_high = prepare(sample_kernel, name="samples")(samples)
    mean, var = fine_x(xs[0])
    (column,) = join([three, *far], mean)
    up, down = along_y(column, 1), along_y(column, -1)
    x_low = lax.ppermute(x_low, "rows", forward)
    x_high = lax.ppermute(x_high, "rows", backward)
    first, second = cut(up, down)
    far = [along_y(first, 1), along_y(second, -1)]
    stats = rest_x(xs, x_low, x_high)
    (whole,) = join([column, up, *far, down])
    *ts, low, high = prepare(truth_kernel, name="truth", in_specs=[VMEM, ANYWHERE])(whole, stats[4])
    low = lax.ppermute(low, "rows", forward)
    high = lax.ppermute(high, "rows", backward)
    fine = fine_t(xs[0], ts[0], mean, var)
    return rest(xs, ts, (x_low, x_high, low, high), stats, fine)


def solution(mesh):
    placed = (P("samp", "rows", None), P("rows", "samp"))
    return jax.shard_map(
        local,
        mesh=mesh,
        in_specs=placed,
        out_specs=(P("samp", "rows", None),) * 5,
        check_vma=False,
    )
```

time: 71.6 us -> 64.2 us (0.90)
  waiting for transfers between devices: 10.2 us -> 7.55 us
  starting transfers between devices: 33.4 us -> 31.2 us
  Pallas kernels: 23.6 us -> 22 us
  other arithmetic: 1.6 us -> 0 us
  local copies, waits for them, and re-layouts: 1.47 us -> 2.24 us
    ppermute x1, starting transfers between devices: 6.34 us -> 1.92 us  [local(): x_high = lax.ppermute(x_high, 'rows', backward)]
    ppermute x1, starting transfers between devices: 3.02 us -> 6.29 us  [local(): x_low = lax.ppermute(x_low, 'rows', forward)]
    ppermute x4, waiting for transfers between devices: 1.68 us -> 0.01 us  [along_y(): return lax.ppermute(x, 'samp', shifted(4, 1, k))]
    concatenate x2 -> x0, other arithmetic: 1.6 us -> none  [local(): jnp.concatenate([packed, along_z(packed, 1), along_z(packed, -1)], axis=0)]
    pallas_call x1, Pallas kernels: 1.66 us -> 0.15 us  [local(): pl.pallas_call(pack_kernel, out_shape=jax.ShapeDtypeStruct((88, 128), f32...]
    ppermute x1, waiting for transfers between devices: 1.43 us -> 2.89 us  [local(): x_high = lax.ppermute(x_high, 'rows', backward)]
    ppermute x4, waiting for transfers between devices: 5.41 us -> 4.11 us  [along_z(): return lax.ppermute(x, 'samp', shifted(8, 4, k))]
    ppermute x1, waiting for transfers between devices: 0.89 us -> 0.01 us  [local(): x_low = lax.ppermute(x_low, 'rows', forward)]
  transfers between devices with their start and end apart: 12 -> 12, of which waited for: 8 -> 4; matrix products, arithmetic and copies ran while one was open for 1% -> 0% of each run, Pallas kernels for 19% -> 21%
where the time goes in v3:
time: 64.2 us; the launch traced here: 64 us
  starting transfers between devices  31.2 us (49%)
  Pallas kernels  22 us (34%)
  waiting for transfers between devices  7.55 us (12%)
  local copies, waits for them, and re-layouts  2.24 us (3%)
  between operations  0.94 us (1%)
    ppermute x4, starting transfers between devices, along_z(): return lax.ppermute(x, 'samp', shifted(8, 4, k))  11 us
    pallas_call x1, Pallas kernels, rest(): pl.pallas_call(rest_kernel, grid=(1,), out_shape=shapes, in_specs=[VMEM]...  6.34 us
    ppermute x1, starting transfers between devices, local(): x_low = lax.ppermute(x_low, 'rows', forward)  6.29 us
    ppermute x4, starting transfers between devices, along_y(): return lax.ppermute(x, 'samp', shifted(4, 1, k))  6.12 us
    pallas_call x1, Pallas kernels, fine_t(): pl.pallas_call(fine_t_kernel, grid=(STRIPS[0] // CHUNK,), out_shape=jax.S...  5.7 us
    ppermute x4, waiting for transfers between devices, along_z(): return lax.ppermute(x, 'samp', shifted(8, 4, k))  4.11 us
    ppermute x1, starting transfers between devices, local(): low = lax.ppermute(low, 'rows', forward)  3.92 us
    pallas_call x1, Pallas kernels, rest_x(): pl.pallas_call(rest_x_kernel, grid=(1,), out_shape=shapes * 2, in_specs=[...  3.45 us
  transfers between devices with their start and end apart: 12, of which 4 were waited for; matrix products, arithmetic and copies ran while one was open for 0% of the time, Pallas kernels for 21%

profile of v3, /device:TPU:1, one launch (start us, length us, event | category | flops | bytes accessed | tf_op | source)
XLA Modules:
  0.0 64.0 jit_solution(10819417594886742143)
XLA Ops:
  0.6 0.9 %copy-done.1 = f32[80,140]{0,1:T(8,128)S(1)} copy-done((f32[80,140]{0,1:T(8,128)S(1)}, f32[80,140]{0,1:T(8,128)}, u32[]{:S(2)}) %copy-start.1) | copy-done | bytes 44824
  1.5 0.1 pack.1.refs_0_
  1.7 6.5 %collective-permute-start.1 = (f32[88,128]{1,0:T(8,128)S(1)}, f32[88,128]{1,0:T(8,128)S(1)}, u32[]{:S(2)}, u32[]{:S(2)}) collective-permute-start(f32[88,128]{1,0:T(8,128)S(1)} %pack.1.refs_0_), channel_id=1, source_target_pairs={{0,224},{8,232},{16,240},{24,248},{32,0},{40,8},{48,16},{56,24},{6... | collective-permute-start | bytes 135176 | tf_op jit(solution)/shard_map/ppermute | solution.py:440
  8.2 1.1 %collective-permute-done.1.refs_2_ = f32[88,128]{1,0:T(8,128)S(1)} collective-permute-done((f32[88,128]{1,0:T(8,128)S(1)}, f32[88,128]{1,0:T(8,128)S(1)}, u32[]{:S(2)}, u32[]{:S(2)}) %collective-permute-start.1) | collective-permute-done | bytes 45088 | tf_op jit(solution)/shard_map/ppermute | solution.py:440
  9.3 3.0 %collective-permute-done.refs_1_ = f32[88,128]{1,0:T(8,128)S(1)} collective-permute-done((f32[88,128]{1,0:T(8,128)S(1)}, f32[88,128]{1,0:T(8,128)S(1)}, u32[]{:S(2)}, u32[]{:S(2)}) %collective-permute-start) | collective-permute-done | bytes 45088 | tf_op jit(solution)/shard_map/ppermute | solution.py:440
  12.3 0.1 collective-permute-start.2
  12.4 4.5 %collective-permute-start.3 = (f32[176,128]{1,0:T(8,128)S(1)}, f32[176,128]{1,0:T(8,128)S(1)}, u32[]{:S(2)}, u32[]{:S(2)}) collective-permute-start(f32[176,128]{1,0:T(8,128)S(1)} %get-tuple-element.45), channel_id=1, source_target_pairs={{0,160},{8,168},{16,176},{24,184},{32,192},{40,200},{48,208},{56,2... | collective-permute-start | bytes 270344 | tf_op jit(solution)/shard_map/ppermute | solution.py:440
  16.8 1.4 %copy-done = f32[1,80,4480]{2,1,0:T(8,128)S(1)} copy-done((f32[1,80,4480]{2,1,0:T(8,128)S(1)}, f32[1,80,4480]{2,1,0:T(8,128)}, u32[]{:S(2)}) %copy-start) | copy-done | bytes 1433624
  18.2 1.4 %samples.1 = (f32[36,80,128]{2,1,0:T(8,128)S(1)}, f32[19,48,128]{2,1,0:T(8,128)S(1)}, f32[10,32,128]{2,1,0:T(8,128)S(1)}, f32[6,16,128]{2,1,0:T(8,128)S(1)}, f32...) custom-call(f32[1,80,4480]{2,1,0:T(8,128)S(1)} %copy-done), custom_call_target="tpu_custom_call" | custom-call | bytes 200000000 | tf_op jit(solution)/shard_map/samples/pallas_call | solution.py:623
  19.6 3.2 %fine_x.1 = (f32[36,64,128]{2,1,0:T(8,128)S(1)}, f32[36,64,128]{2,1,0:T(8,128)S(1)}) custom-call(f32[36,80,128]{2,1,0:T(8,128)S(1)} %get-tuple-element.46.x_ref.x_next.refs_6_.refs_7_.refs_22_.refs_23_, f32[36,80,128]{2,1,0:T(8,128)S(1)} %get-tuple-element.46.x_ref.x_next.refs_6_.refs_7_.refs_22_.refs_23_), custom_call_target="tpu_custom_call" | custom-call | bytes 250000000 | tf_op jit(solution)/shard_map/fine_x/pallas_call | solution.py:507
  22.8 2.8 %collective-permute-start.5 = (f32[704,128]{1,0:T(8,128)S(1)}, f32[704,128]{1,0:T(8,128)S(1)}, u32[]{:S(2)}, u32[]{:S(2)}) collective-permute-start(f32[704,128]{1,0:T(8,128)S(1)} %join.4.refs_0_), channel_id=1, source_target_pairs={{0,24},{8,0},{16,8},{24,16},{32,56},{40,32},{48,40},{56,48},{64,88... | collective-permute-start | bytes 1081352 | tf_op jit(solution)/shard_map/ppermute | solution.py:444
  25.6 6.3 %collective-permute-start.8 = (f32[75,8,128]{2,1,0:T(8,128)S(1)}, f32[75,8,128]{2,1,0:T(8,128)S(1)}, u32[]{:S(2)}, u32[]{:S(2)}) collective-permute-start(f32[75,8,128]{2,1,0:T(8,128)S(1)} %get-tuple-element.50), channel_id=1, source_target_pairs={{0,1},{1,2},{2,3},{3,4},{4,5},{5,6},{6,7},{8,9},{9,10},{10,11},{11... | collective-permute-start | bytes 921608 | tf_op jit(solution)/shard_map/ppermute | solution.py:627
  31.9 1.9 %collective-permute-start.9 = (f32[75,8,128]{2,1,0:T(8,128)S(1)}, f32[75,8,128]{2,1,0:T(8,128)S(1)}, u32[]{:S(2)}, u32[]{:S(2)}) collective-permute-start(f32[75,8,128]{2,1,0:T(8,128)S(1)} %get-tuple-element.51), channel_id=1, source_target_pairs={{1,0},{2,1},{3,2},{4,3},{5,4},{6,5},{7,6},{9,8},{10,9},{11,10},{12... | collective-permute-start | bytes 921608 | tf_op jit(solution)/shard_map/ppermute | solution.py:628
  33.9 0.4 collective-permute-start.6
  34.3 2.9 %collective-permute-start.7 = (f32[352,128]{1,0:T(8,128)S(1)}, f32[352,128]{1,0:T(8,128)S(1)}, u32[]{:S(2)}, u32[]{:S(2)}) collective-permute-start(f32[352,128]{1,0:T(8,128)S(1)} %get-tuple-element.49), channel_id=1, source_target_pairs={{0,24},{8,0},{16,8},{24,16},{32,56},{40,32},{48,40},{56,48},{64,88... | collective-permute-start | bytes 540680 | tf_op jit(solution)/shard_map/ppermute | solution.py:444
  37.2 2.9 %collective-permute-done.9.refs_5_.refs_9_ = f32[75,8,128]{2,1,0:T(8,128)S(1)} collective-permute-done((f32[75,8,128]{2,1,0:T(8,128)S(1)}, f32[75,8,128]{2,1,0:T(8,128)S(1)}, u32[]{:S(2)}, u32[]{:S(2)}) %collective-permute-start.9) | collective-permute-done | bytes 307232 | tf_op jit(solution)/shard_map/ppermute | solution.py:628
  40.1 3.5 %rest_x.1 = (f32[35,16,128]{2,1,0:T(8,128)S(1)}, f32[18,48,128]{2,1,0:T(8,128)S(1)}, f32[9,32,128]{2,1,0:T(8,128)S(1)}, f32[5,16,128]{2,1,0:T(8,128)S(1)}, f32[3...) custom-call(f32[19,48,128]{2,1,0:T(8,128)S(1)} %get-tuple-element.40, ...), custom_call_target="tpu_custom_call" | custom-call | bytes 250000000 | tf_op jit(solution)/shard_map/rest_x/pallas_call | solution.py:553
  43.5 0.1 join.5.g_ref
  43.6 1.7 %truth.1 = (f32[36,80,128]{2,1,0:T(8,128)S(1)}, f32[19,48,128]{2,1,0:T(8,128)S(1)}, f32[10,32,128]{2,1,0:T(8,128)S(1)}, f32[6,16,128]{2,1,0:T(8,128)S(1)}, f32[4...) custom-call(f32[2816,128]{1,0:T(8,128)S(1)} %join.5.g_ref, ...), custom_call_target="tpu_custom_call" | custom-call | bytes 200000000 | tf_op jit(solution)/shard_map/truth/pallas_call | solution.py:633
  45.4 3.9 %collective-permute-start.10 = (f32[75,8,128]{2,1,0:T(8,128)S(1)}, f32[75,8,128]{2,1,0:T(8,128)S(1)}, u32[]{:S(2)}, u32[]{:S(2)}) collective-permute-start(f32[75,8,128]{2,1,0:T(8,128)S(1)} %get-tuple-element.57), channel_id=1, source_target_pairs={{0,1},{1,2},{2,3},{3,4},{4,5},{5,6},{6,7},{8,9},{9,10},{10,11},{11... | collective-permute-start | bytes 921608 | tf_op jit(solution)/shard_map/ppermute | solution.py:634
  49.3 1.9 %collective-permute-start.11 = (f32[75,8,128]{2,1,0:T(8,128)S(1)}, f32[75,8,128]{2,1,0:T(8,128)S(1)}, u32[]{:S(2)}, u32[]{:S(2)}) collective-permute-start(f32[75,8,128]{2,1,0:T(8,128)S(1)} %get-tuple-element.58), channel_id=1, source_target_pairs={{1,0},{2,1},{3,2},{4,3},{5,4},{6,5},{7,6},{9,8},{10,9},{11,10},{12... | collective-permute-start | bytes 921608 | tf_op jit(solution)/shard_map/ppermute | solution.py:635
  51.2 5.7 %fine_t.1.refs_26_ = f32[1,80,4480]{2,1,0:T(8,128)} custom-call(f32[36,80,128]{2,1,0:T(8,128)S(1)} %get-tuple-element.46.x_ref.x_next.refs_6_.refs_7_.refs_22_.refs_23_, f32[36,80,128]{2,1,0:T(8,128)S(1)} %get-tuple-element.46.x_ref.x_next.refs_6_.refs_7_.refs_22_.refs_23_, f32[36,80,128]{2,1,0:T(8,128)S(1)} %get-tuple-element.68.t_ref.t_next.refs_24_.refs_25_, ...), custom_call_target="tpu_custom_call" | custom-call | bytes 400000000 | tf_op jit(solution)/shard_map/fine_t/pallas_call | solution.py:526
  56.9 0.5 collective-permute-done.11.refs_11_
  57.5 6.3 %rest.1 = (f32[1,80,4480]{2,1,0:T(8,128)}, f32[1,40,2240]{2,1,0:T(8,128)}, f32[20,1,1120]{2,1,0:T(1,128)}, f32[10,1,560]{2,1,0:T(1,128)}, f32[5,1,280]{2,1,0:T(1,128)}) custom-call(f32[19,48,128]{2,1,0:T(8,128)S(1)} %get-tuple-element.40.refs_0_, f32[10,32,128]{2,1,0:T(8,128)S(1)} %get-tuple-element.41.refs_1_, ...), custom_call_target="tpu_custom_call", output_to_operand_aliasing={{0}: (26, {})} | custom-call | tf_op jit(solution)/shard_map/rest/pallas_call | solution.py:577
  (15 shorter events, 0.1 us)
Async XLA Ops:
  0.6 0.9 %copy-start.1 = (f32[80,140]{0,1:T(8,128)S(1)}, f32[80,140]{0,1:T(8,128)}, u32[]{:S(2)}) copy-start(f32[80,140]{0,1:T(8,128)} %param.3) | copy-start | bytes 134404
  1.7 7.6 %collective-permute-start.1 = (f32[88,128]{1,0:T(8,128)S(1)}, f32[88,128]{1,0:T(8,128)S(1)}, u32[]{:S(2)}, u32[]{:S(2)}) collective-permute-start(f32[88,128]{1,0:T(8,128)S(1)} %pack.1.refs_0_), channel_id=1, source_target_pairs={{0,224},{8,232},{16,240},{24,248},{32,0},{40,8},{48,16},{56,24},{6... | collective-permute-start | bytes 135176 | tf_op jit(solution)/shard_map/ppermute | solution.py:440
  8.2 4.1 %collective-permute-start = (f32[88,128]{1,0:T(8,128)S(1)}, f32[88,128]{1,0:T(8,128)S(1)}, u32[]{:S(2)}, u32[]{:S(2)}) collective-permute-start(f32[88,128]{1,0:T(8,128)S(1)} %pack.1.refs_0_), channel_id=1, source_target_pairs={{0,32},{8,40},{16,48},{24,56},{32,64},{40,72},{48,80},{56,88},{64,... | collective-permute-start | bytes 135176 | tf_op jit(solution)/shard_map/ppermute | solution.py:440
  12.3 10.5 %collective-permute-start.2 = (f32[264,128]{1,0:T(8,128)S(1)}, f32[264,128]{1,0:T(8,128)S(1)}, u32[]{:S(2)}, u32[]{:S(2)}) collective-permute-start(f32[264,128]{1,0:T(8,128)S(1)} %get-tuple-element.44.refs_0_), channel_id=1, source_target_pairs={{0,96},{8,104},{16,112},{24,120},{32,128},{40,136},{48,144},{56,15... | collective-permute-start | bytes 405512 | tf_op jit(solution)/shard_map/ppermute | solution.py:440
  12.4 10.4 %collective-permute-start.3 = (f32[176,128]{1,0:T(8,128)S(1)}, f32[176,128]{1,0:T(8,128)S(1)}, u32[]{:S(2)}, u32[]{:S(2)}) collective-permute-start(f32[176,128]{1,0:T(8,128)S(1)} %get-tuple-element.45), channel_id=1, source_target_pairs={{0,160},{8,168},{16,176},{24,184},{32,192},{40,200},{48,208},{56,2... | collective-permute-start | bytes 270344 | tf_op jit(solution)/shard_map/ppermute | solution.py:440
  16.8 1.4 %copy-start = (f32[1,80,4480]{2,1,0:T(8,128)S(1)}, f32[1,80,4480]{2,1,0:T(8,128)}, u32[]{:S(2)}) copy-start(f32[1,80,4480]{2,1,0:T(8,128)} %x_ref.1) | copy-start | bytes 4300804
  22.8 11.0 %collective-permute-start.5 = (f32[704,128]{1,0:T(8,128)S(1)}, f32[704,128]{1,0:T(8,128)S(1)}, u32[]{:S(2)}, u32[]{:S(2)}) collective-permute-start(f32[704,128]{1,0:T(8,128)S(1)} %join.4.refs_0_), channel_id=1, source_target_pairs={{0,24},{8,0},{16,8},{24,16},{32,56},{40,32},{48,40},{56,48},{64,88... | collective-permute-start | bytes 1081352 | tf_op jit(solution)/shard_map/ppermute | solution.py:444
  25.6 8.2 %collective-permute-start.4 = (f32[704,128]{1,0:T(8,128)S(1)}, f32[704,128]{1,0:T(8,128)S(1)}, u32[]{:S(2)}, u32[]{:S(2)}) collective-permute-start(f32[704,128]{1,0:T(8,128)S(1)} %join.4.refs_0_), channel_id=1, source_target_pairs={{0,8},{8,16},{16,24},{24,0},{32,40},{40,48},{48,56},{56,32},{64,72... | collective-permute-start | bytes 1081352 | tf_op jit(solution)/shard_map/ppermute | solution.py:444
  25.6 11.6 %collective-permute-start.8 = (f32[75,8,128]{2,1,0:T(8,128)S(1)}, f32[75,8,128]{2,1,0:T(8,128)S(1)}, u32[]{:S(2)}, u32[]{:S(2)}) collective-permute-start(f32[75,8,128]{2,1,0:T(8,128)S(1)} %get-tuple-element.50), channel_id=1, source_target_pairs={{0,1},{1,2},{2,3},{3,4},{4,5},{5,6},{6,7},{8,9},{9,10},{10,11},{11... | collective-permute-start | bytes 921608 | tf_op jit(solution)/shard_map/ppermute | solution.py:627
  31.9 8.2 %collective-permute-start.9 = (f32[75,8,128]{2,1,0:T(8,128)S(1)}, f32[75,8,128]{2,1,0:T(8,128)S(1)}, u32[]{:S(2)}, u32[]{:S(2)}) collective-permute-start(f32[75,8,128]{2,1,0:T(8,128)S(1)} %get-tuple-element.51), channel_id=1, source_target_pairs={{1,0},{2,1},{3,2},{4,3},{5,4},{6,5},{7,6},{9,8},{10,9},{11,10},{12... | collective-permute-start | bytes 921608 | tf_op jit(solution)/shard_map/ppermute | solution.py:628
  33.9 9.7 %collective-permute-start.6 = (f32[352,128]{1,0:T(8,128)S(1)}, f32[352,128]{1,0:T(8,128)S(1)}, u32[]{:S(2)}, u32[]{:S(2)}) collective-permute-start(f32[352,128]{1,0:T(8,128)S(1)} %get-tuple-element.48), channel_id=1, source_target_pairs={{0,8},{8,16},{16,24},{24,0},{32,40},{40,48},{48,56},{56,32},{64,72... | collective-permute-start | bytes 540680 | tf_op jit(solution)/shard_map/ppermute | solution.py:444
  34.3 9.3 %collective-permute-start.7 = (f32[352,128]{1,0:T(8,128)S(1)}, f32[352,128]{1,0:T(8,128)S(1)}, u32[]{:S(2)}, u32[]{:S(2)}) collective-permute-start(f32[352,128]{1,0:T(8,128)S(1)} %get-tuple-element.49), channel_id=1, source_target_pairs={{0,24},{8,0},{16,8},{24,16},{32,56},{40,32},{48,40},{56,48},{64,88... | collective-permute-start | bytes 540680 | tf_op jit(solution)/shard_map/ppermute | solution.py:444
  45.4 11.6 %collective-permute-start.10 = (f32[75,8,128]{2,1,0:T(8,128)S(1)}, f32[75,8,128]{2,1,0:T(8,128)S(1)}, u32[]{:S(2)}, u32[]{:S(2)}) collective-permute-start(f32[75,8,128]{2,1,0:T(8,128)S(1)} %get-tuple-element.57), channel_id=1, source_target_pairs={{0,1},{1,2},{2,3},{3,4},{4,5},{5,6},{6,7},{8,9},{9,10},{10,11},{11... | collective-permute-start | bytes 921608 | tf_op jit(solution)/shard_map/ppermute | solution.py:634
  49.3 8.2 %collective-permute-start.11 = (f32[75,8,128]{2,1,0:T(8,128)S(1)}, f32[75,8,128]{2,1,0:T(8,128)S(1)}, u32[]{:S(2)}, u32[]{:S(2)}) collective-permute-start(f32[75,8,128]{2,1,0:T(8,128)S(1)} %get-tuple-element.58), channel_id=1, source_target_pairs={{1,0},{2,1},{3,2},{4,3},{5,4},{6,5},{7,6},{9,8},{10,9},{11,10},{12... | collective-permute-start | bytes 921608 | tf_op jit(solution)/shard_map/ppermute | solution.py:635
